TPU v7x, 512 devices: a whole 4x8x8 slice. The times are simulated.
512 devices in a mesh: band: 8 (over y_lo, core), grid: 64 (over y_hi, x, z).
Axes of the slice: x: 4, y: 8 (y_hi: 2, y_lo: 4; y = y_hi * 4 + y_lo), z: 8, core: 2. Of those that a mesh axis runs over, the one named last changes fastest.
Arguments:
- orbitals: float32 [8, 2, 192, 192, 192], P('band', None, 'grid'), may hold values from -6 to 6
- occupations: float32 [8], P('band'), may hold values from 0.5 to 2
- ion_potential: float32 [192, 192, 192], P('grid'), may hold values from -0.6 to 0.6
- hxc_potential: float32 [192, 192, 192], P('grid'), may hold values from -0.4 to 0.4
Outputs:
- new_orbitals: float32 [8, 2, 192, 192, 192], P('band', None, 'grid')
- new_potential: float32 [192, 192, 192], P('grid')
All inputs are finite; a program needn't handle non-finite values.
Results may differ from a plain program's by a relative error of at most 0.0003.
Values sent between devices are 32-bit elements; how exact they have to be, the bound alone decides.
A program may use at most 64 MiB of HBM per device.

v0:
```python
import math

import jax
import jax.numpy as jnp
from jax import lax
from jax.sharding import PartitionSpec as P

BESSEL_ZERO = 0.8462873527504802
BESSEL_ONE = 0.36884204609417703
BESSEL_TWO = 0.07581776248
XC_FACTOR = 0.98474502


def tables(length):
    idx = jnp.arange(length, dtype=jnp.int32)
    angle = (idx[:, None] * idx[None, :] % length).astype(jnp.float32) * (2.0 * math.pi / length)
    return (jnp.cos(angle), jnp.sin(angle))


def transform(real_part, imag_part, form, inverse, length):
    cosine, sine = tables(length)
    high = lax.Precision.HIGHEST
    rc = jnp.einsum(form, real_part, cosine, precision=high)
    rs = jnp.einsum(form, real_part, sine, precision=high)
    ic = jnp.einsum(form, imag_part, cosine, precision=high)
    isn = jnp.einsum(form, imag_part, sine, precision=high)
    if inverse:
        scale = 1.0 / length
        return ((rc - isn) * scale, (ic + rs) * scale)
    return (rc + isn, ic - rs)


def along_z(real_part, imag_part, inverse):
    return transform(real_part, imag_part, "oxyn,nk->oxyk", inverse, real_part.shape[3])


def along_y(real_part, imag_part, inverse):
    return transform(real_part, imag_part, "oxnz,nk->oxkz", inverse, real_part.shape[2])


def along_x(real_part, imag_part, inverse):
    return transform(real_part, imag_part, "onyz,nk->okyz", inverse, real_part.shape[1])


def forward(real_part, imag_part):
    real_part, imag_part = along_z(real_part, imag_part, False)
    real_part, imag_part = along_y(real_part, imag_part, False)
    real_part, imag_part = (
        lax.all_to_all(real_part, "grid", split_axis=2, concat_axis=1, tiled=True),
        lax.all_to_all(imag_part, "grid", split_axis=2, concat_axis=1, tiled=True),
    )
    return along_x(real_part, imag_part, False)


def backward(real_part, imag_part):
    real_part, imag_part = along_x(real_part, imag_part, True)
    real_part, imag_part = (
        lax.all_to_all(real_part, "grid", split_axis=1, concat_axis=2, tiled=True),
        lax.all_to_all(imag_part, "grid", split_axis=1, concat_axis=2, tiled=True),
    )
    real_part, imag_part = along_y(real_part, imag_part, True)
    real_part, imag_part = along_z(real_part, imag_part, True)
    return (real_part, imag_part)


def frequency(idx, length):
    return jnp.where(idx < length // 2, idx, idx - length).astype(jnp.float32)


def squares_block(x_count, y_start, y_count, length):
    fx = frequency(jnp.arange(x_count, dtype=jnp.int32), length)
    fy = frequency(y_start + jnp.arange(y_count, dtype=jnp.int32), length)
    fz = frequency(jnp.arange(length, dtype=jnp.int32), length)
    return (fx * fx)[:, None, None] + (fy * fy)[None, :, None] + (fz * fz)[None, None, :]


def hartree_filter(squares, length):
    return jnp.where(squares > 0, length * math.sqrt(length) / 16.0 / (squares + 1.0), 0.0)


def local(orbitals, occupations, ion_potential, hxc_potential):
    length = orbitals.shape[-1]
    columns = length // lax.axis_size("grid")
    grid_pos = lax.axis_index("grid")
    squares = squares_block(length, grid_pos * columns, columns, length)
    kinetic = 2.0 * squares / (3.0 * (length / 2) ** 2) - 1.0
    potential = ion_potential + hxc_potential

    def hamilton(real_part, imag_part):
        fre, fim = forward(real_part, imag_part)
        back_re, back_im = backward(kinetic * fre, kinetic * fim)
        return (back_re + potential * real_part, back_im + potential * imag_part)

    psi_re = orbitals[:, 0]
    psi_im = orbitals[:, 1]
    first_re, first_im = hamilton(psi_re, psi_im)
    again_re, again_im = hamilton(first_re, first_im)
    second_re = 2.0 * again_re - psi_re
    second_im = 2.0 * again_im - psi_im
    fresh_re = BESSEL_ZERO * psi_re + 2.0 * BESSEL_ONE * first_im - 2.0 * BESSEL_TWO * second_re
    fresh_im = BESSEL_ZERO * psi_im - 2.0 * BESSEL_ONE * first_re - 2.0 * BESSEL_TWO * second_im
    new_orbitals = jnp.stack([fresh_re, fresh_im], axis=1)
    partial_value = jnp.sum(
        occupations[:, None, None, None] * (fresh_re * fresh_re + fresh_im * fresh_im), axis=0
    )
    density = lax.psum(partial_value, "band")
    fre, fim = forward(density[None], jnp.zeros_like(density)[None])
    kernel = hartree_filter(squares, length)
    hart_re, hart_im = backward(kernel * fre, kernel * fim)
    new_potential = hart_re[0] - XC_FACTOR * jnp.cbrt(density)
    return (new_orbitals, new_potential)


def solution(mesh):
    placed = (
        P("band", None, "grid", None, None),
        P("band"),
        P("grid", None, None),
        P("grid", None, None),
    )
    return jax.shard_map(
        local,
        mesh=mesh,
        in_specs=placed,
        out_specs=(P("band", None, "grid", None, None), P("grid", None, None)),
        check_vma=False,
    )
```

profile of v0, /device:TPU:6, one launch (start us, length us, event | category | flops | bytes accessed | tf_op | source)
XLA Modules:
  0.0 574.1 jit_solution(15256407723588242375)
XLA Ops:
  7.2 3.1 fusion.63
  21.9 19.1 %all-to-all-start = ((f32[1,3,192,192]{3,0,1,2:T(1,128)}), f32[1,3,192,192]{3,0,1,2:T(1,128)S(1)}, u32[]{:S(2)}, u32[]{:S(2)}) async-start(f32[1,3,192,192]{3,0,1,2:T(1,128)} %copy.242), calls=%async_computation | async-start | bytes 1179648 | tf_op jit(solution)/shard_map/all_to_all | solution.py:50
  46.4 14.3 %all-to-all-done = f32[1,3,192,192]{3,0,1,2:T(1,128)S(1)} async-done(((f32[1,3,192,192]{3,0,1,2:T(1,128)}), f32[1,3,192,192]{3,0,1,2:T(1,128)S(1)}, u32[]{:S(2)}, u32[]{:S(2)}) %all-to-all-start) | async-done | bytes 442400 | tf_op jit(solution)/shard_map/all_to_all | solution.py:50
  60.7 9.9 %all-to-all-start.1 = ((f32[1,3,192,192]{3,0,1,2:T(1,128)}), f32[1,3,192,192]{3,0,1,2:T(1,128)S(1)}, u32[]{:S(2)}, u32[]{:S(2)}) async-start(f32[1,3,192,192]{3,0,1,2:T(1,128)} %copy.250), calls=%async_computation.1 | async-start | bytes 1179648 | tf_op jit(solution)/shard_map/all_to_all | solution.py:49
  71.8 19.9 %all-to-all-done.1 = f32[1,3,192,192]{3,0,1,2:T(1,128)S(1)} async-done(((f32[1,3,192,192]{3,0,1,2:T(1,128)}), f32[1,3,192,192]{3,0,1,2:T(1,128)S(1)}, u32[]{:S(2)}, u32[]{:S(2)}) %all-to-all-start.1) | async-done | bytes 442400 | tf_op jit(solution)/shard_map/all_to_all | solution.py:49
  105.0 7.8 %all-to-all-start.3 = ((f32[1,192,3,192]{3,0,2,1:T(1,128)}), f32[1,192,3,192]{3,0,2,1:T(1,128)S(1)}, u32[]{:S(2)}, u32[]{:S(2)}) async-start(f32[1,192,3,192]{3,0,2,1:T(1,128)} %copy.263), calls=%async_computation.3 | async-start | bytes 1179648 | tf_op jit(solution)/shard_map/all_to_all | solution.py:58
  117.1 16.8 %all-to-all-done.3 = f32[1,192,3,192]{3,0,2,1:T(1,128)S(1)} async-done(((f32[1,192,3,192]{3,0,2,1:T(1,128)}), f32[1,192,3,192]{3,0,2,1:T(1,128)S(1)}, u32[]{:S(2)}, u32[]{:S(2)}) %all-to-all-start.3) | async-done | bytes 442400 | tf_op jit(solution)/shard_map/all_to_all | solution.py:58
  133.9 7.9 %all-to-all-start.2 = ((f32[1,192,3,192]{3,0,2,1:T(1,128)}), f32[1,192,3,192]{3,0,2,1:T(1,128)}, u32[]{:S(2)}, u32[]{:S(2)}) async-start(f32[1,192,3,192]{3,0,2,1:T(1,128)} %copy.258), calls=%async_computation.2 | async-start | bytes 1179648 | tf_op jit(solution)/shard_map/all_to_all | solution.py:59
  143.6 19.3 %all-to-all-done.2 = f32[1,192,3,192]{3,0,2,1:T(1,128)} async-done(((f32[1,192,3,192]{3,0,2,1:T(1,128)}), f32[1,192,3,192]{3,0,2,1:T(1,128)}, u32[]{:S(2)}, u32[]{:S(2)}) %all-to-all-start.2) | async-done | bytes 442400 | tf_op jit(solution)/shard_map/all_to_all | solution.py:59
  188.9 8.1 %all-to-all-start.4 = ((f32[1,3,192,192]{3,0,1,2:T(1,128)}), f32[1,3,192,192]{3,0,1,2:T(1,128)}, u32[]{:S(2)}, u32[]{:S(2)}) async-start(f32[1,3,192,192]{3,0,1,2:T(1,128)} %copy.270), calls=%async_computation.4 | async-start | bytes 1179648 | tf_op jit(solution)/shard_map/all_to_all | solution.py:49
  201.4 16.4 %all-to-all-done.4 = f32[1,3,192,192]{3,0,1,2:T(1,128)} async-done(((f32[1,3,192,192]{3,0,1,2:T(1,128)}), f32[1,3,192,192]{3,0,1,2:T(1,128)}, u32[]{:S(2)}, u32[]{:S(2)}) %all-to-all-start.4) | async-done | bytes 442400 | tf_op jit(solution)/shard_map/all_to_all | solution.py:49
  217.8 8.1 %all-to-all-start.5 = ((f32[1,3,192,192]{3,0,1,2:T(1,128)}), f32[1,3,192,192]{3,0,1,2:T(1,128)}, u32[]{:S(2)}, u32[]{:S(2)}) async-start(f32[1,3,192,192]{3,0,1,2:T(1,128)} %copy.276), calls=%async_computation.5 | async-start | bytes 1179648 | tf_op jit(solution)/shard_map/all_to_all | solution.py:50
  230.1 16.8 %all-to-all-done.5 = f32[1,3,192,192]{3,0,1,2:T(1,128)} async-done(((f32[1,3,192,192]{3,0,1,2:T(1,128)}), f32[1,3,192,192]{3,0,1,2:T(1,128)}, u32[]{:S(2)}, u32[]{:S(2)}) %all-to-all-start.5) | async-done | bytes 442400 | tf_op jit(solution)/shard_map/all_to_all | solution.py:50
  255.8 2.6 fusion.34
  264.2 8.2 %all-to-all-start.7 = ((f32[1,192,3,192]{3,0,2,1:T(1,128)}), f32[1,192,3,192]{3,0,2,1:T(1,128)}, u32[]{:S(2)}, u32[]{:S(2)}) async-start(f32[1,192,3,192]{3,0,2,1:T(1,128)} %copy.289), calls=%async_computation.7 | async-start | bytes 1179648 | tf_op jit(solution)/shard_map/all_to_all | solution.py:59
  272.5 2.5 fusion.139
  277.9 15.7 %all-to-all-done.7 = f32[1,192,3,192]{3,0,2,1:T(1,128)} async-done(((f32[1,192,3,192]{3,0,2,1:T(1,128)}), f32[1,192,3,192]{3,0,2,1:T(1,128)}, u32[]{:S(2)}, u32[]{:S(2)}) %all-to-all-start.7) | async-done | bytes 442400 | tf_op jit(solution)/shard_map/all_to_all | solution.py:59
  293.6 7.9 %all-to-all-start.6 = ((f32[1,192,3,192]{3,0,2,1:T(1,128)}), f32[1,192,3,192]{3,0,2,1:T(1,128)}, u32[]{:S(2)}, u32[]{:S(2)}) async-start(f32[1,192,3,192]{3,0,2,1:T(1,128)} %copy.284), calls=%async_computation.6 | async-start | bytes 1179648 | tf_op jit(solution)/shard_map/all_to_all | solution.py:58
  305.8 16.7 %all-to-all-done.6 = f32[1,192,3,192]{3,0,2,1:T(1,128)} async-done(((f32[1,192,3,192]{3,0,2,1:T(1,128)}), f32[1,192,3,192]{3,0,2,1:T(1,128)}, u32[]{:S(2)}, u32[]{:S(2)}) %all-to-all-start.6) | async-done | bytes 442400 | tf_op jit(solution)/shard_map/all_to_all | solution.py:58
  326.9 2.5 fusion.141
  338.1 2.8 add_multiply_fusion.1
  342.3 70.0 %all-reduce.2.cloned.1.call-done = f32[3,192,192]{2,1,0:T(8,128)} async-done(((f32[3,192,192]{2,1,0:T(8,128)}), f32[3,192,192]{2,1,0:T(8,128)}) %all-reduce.2.cloned.1.call-update) | async-done | bytes 442384 | tf_op jit(solution)/shard_map/psum | solution.py:106
  412.3 2.5 fusion.148
  421.9 14.0 %all-to-all-start.9 = ((f32[1,3,192,192]{3,0,1,2:T(1,128)}), f32[1,3,192,192]{3,0,1,2:T(1,128)}, u32[]{:S(2)}, u32[]{:S(2)}) async-start(f32[1,3,192,192]{3,0,1,2:T(1,128)} %copy.302), calls=%async_computation.9 | async-start | bytes 1179648 | tf_op jit(solution)/shard_map/all_to_all | solution.py:50
  440.2 16.0 %all-to-all-done.9 = f32[1,3,192,192]{3,0,1,2:T(1,128)} async-done(((f32[1,3,192,192]{3,0,1,2:T(1,128)}), f32[1,3,192,192]{3,0,1,2:T(1,128)}, u32[]{:S(2)}, u32[]{:S(2)}) %all-to-all-start.9) | async-done | bytes 442400 | tf_op jit(solution)/shard_map/all_to_all | solution.py:50
  456.2 8.1 %all-to-all-start.8 = ((f32[1,3,192,192]{3,0,1,2:T(1,128)}), f32[1,3,192,192]{3,0,1,2:T(1,128)S(1)}, u32[]{:S(2)}, u32[]{:S(2)}) async-start(f32[1,3,192,192]{3,0,1,2:T(1,128)} %copy.296), calls=%async_computation.8 | async-start | bytes 1179648 | tf_op jit(solution)/shard_map/all_to_all | solution.py:49
  466.5 19.1 %all-to-all-done.8 = f32[1,3,192,192]{3,0,1,2:T(1,128)S(1)} async-done(((f32[1,3,192,192]{3,0,1,2:T(1,128)}), f32[1,3,192,192]{3,0,1,2:T(1,128)S(1)}, u32[]{:S(2)}, u32[]{:S(2)}) %all-to-all-start.8) | async-done | bytes 442400 | tf_op jit(solution)/shard_map/all_to_all | solution.py:49
  496.9 7.8 %all-to-all-start.10 = ((f32[1,192,3,192]{3,0,2,1:T(1,128)}), f32[1,192,3,192]{3,0,2,1:T(1,128)}, u32[]{:S(2)}, u32[]{:S(2)}) async-start(f32[1,192,3,192]{3,0,2,1:T(1,128)} %copy.310), calls=%async_computation.10 | async-start | bytes 1179648 | tf_op jit(solution)/shard_map/all_to_all | solution.py:58
  509.1 16.9 %all-to-all-done.10 = f32[1,192,3,192]{3,0,2,1:T(1,128)} async-done(((f32[1,192,3,192]{3,0,2,1:T(1,128)}), f32[1,192,3,192]{3,0,2,1:T(1,128)}, u32[]{:S(2)}, u32[]{:S(2)}) %all-to-all-start.10) | async-done | bytes 442400 | tf_op jit(solution)/shard_map/all_to_all | solution.py:58
  526.0 7.6 %all-to-all-start.11 = ((f32[1,192,3,192]{3,0,2,1:T(1,128)}), f32[1,192,3,192]{3,0,2,1:T(1,128)S(1)}, u32[]{:S(2)}, u32[]{:S(2)}) async-start(f32[1,192,3,192]{3,0,2,1:T(1,128)} %copy.315), calls=%async_computation.11 | async-start | bytes 1179648 | tf_op jit(solution)/shard_map/all_to_all | solution.py:59
  536.3 18.7 %all-to-all-done.11 = f32[1,192,3,192]{3,0,2,1:T(1,128)S(1)} async-done(((f32[1,192,3,192]{3,0,2,1:T(1,128)}), f32[1,192,3,192]{3,0,2,1:T(1,128)S(1)}, u32[]{:S(2)}, u32[]{:S(2)}) %all-to-all-start.11) | async-done | bytes 442400 | tf_op jit(solution)/shard_map/all_to_all | solution.py:59
  564.5 2.6 fusion.1
  (142 shorter events, 148.5 us)
Async XLA Ops:
  7.2 3.1 copy-start
  21.9 38.8 %all-to-all-start = ((f32[1,3,192,192]{3,0,1,2:T(1,128)}), f32[1,3,192,192]{3,0,1,2:T(1,128)S(1)}, u32[]{:S(2)}, u32[]{:S(2)}) async-start(f32[1,3,192,192]{3,0,1,2:T(1,128)} %copy.242), calls=%async_computation | async-start | bytes 1179648 | tf_op jit(solution)/shard_map/all_to_all | solution.py:50
  60.7 31.1 %all-to-all-start.1 = ((f32[1,3,192,192]{3,0,1,2:T(1,128)}), f32[1,3,192,192]{3,0,1,2:T(1,128)S(1)}, u32[]{:S(2)}, u32[]{:S(2)}) async-start(f32[1,3,192,192]{3,0,1,2:T(1,128)} %copy.250), calls=%async_computation.1 | async-start | bytes 1179648 | tf_op jit(solution)/shard_map/all_to_all | solution.py:49
  105.0 29.0 %all-to-all-start.3 = ((f32[1,192,3,192]{3,0,2,1:T(1,128)}), f32[1,192,3,192]{3,0,2,1:T(1,128)S(1)}, u32[]{:S(2)}, u32[]{:S(2)}) async-start(f32[1,192,3,192]{3,0,2,1:T(1,128)} %copy.263), calls=%async_computation.3 | async-start | bytes 1179648 | tf_op jit(solution)/shard_map/all_to_all | solution.py:58
  115.7 26.2 %copy-start.13 = (f32[3,192,192]{2,1,0:T(8,128)S(1)}, f32[3,192,192]{2,1,0:T(8,128)}, u32[]{:S(2)}) copy-start(f32[3,192,192]{2,1,0:T(8,128)} %param.6) | copy-start | bytes 1327108
  115.7 26.2 %copy-start.14 = (f32[3,192,192]{2,1,0:T(8,128)S(1)}, f32[3,192,192]{2,1,0:T(8,128)}, u32[]{:S(2)}) copy-start(f32[3,192,192]{2,1,0:T(8,128)} %param.7) | copy-start | bytes 1327108
  133.9 8.0 %copy-start.8 = (f32[1,192,3,192]{3,0,2,1:T(1,128)}, f32[1,192,3,192]{3,0,2,1:T(1,128)S(1)}, u32[]{:S(2)}) copy-start(f32[1,192,3,192]{3,0,2,1:T(1,128)S(1)} %all-to-all-done.3) | copy-start | bytes 1327108
  133.9 29.0 %all-to-all-start.2 = ((f32[1,192,3,192]{3,0,2,1:T(1,128)}), f32[1,192,3,192]{3,0,2,1:T(1,128)}, u32[]{:S(2)}, u32[]{:S(2)}) async-start(f32[1,192,3,192]{3,0,2,1:T(1,128)} %copy.258), calls=%async_computation.2 | async-start | bytes 1179648 | tf_op jit(solution)/shard_map/all_to_all | solution.py:59
  183.8 0.8 copy-start.1
  188.9 28.9 %all-to-all-start.4 = ((f32[1,3,192,192]{3,0,1,2:T(1,128)}), f32[1,3,192,192]{3,0,1,2:T(1,128)}, u32[]{:S(2)}, u32[]{:S(2)}) async-start(f32[1,3,192,192]{3,0,1,2:T(1,128)} %copy.270), calls=%async_computation.4 | async-start | bytes 1179648 | tf_op jit(solution)/shard_map/all_to_all | solution.py:49
  197.0 1.4 copy-start.2
  217.8 29.1 %all-to-all-start.5 = ((f32[1,3,192,192]{3,0,1,2:T(1,128)}), f32[1,3,192,192]{3,0,1,2:T(1,128)}, u32[]{:S(2)}, u32[]{:S(2)}) async-start(f32[1,3,192,192]{3,0,1,2:T(1,128)} %copy.276), calls=%async_computation.5 | async-start | bytes 1179648 | tf_op jit(solution)/shard_map/all_to_all | solution.py:50
  230.1 24.3 %copy-start.5 = (f32[192,3,192]{2,0,1:T(8,128)}, f32[192,3,192]{2,0,1:T(8,128)S(1)}, u32[]{:S(2)}) copy-start(f32[192,3,192]{2,0,1:T(8,128)S(1)} %reshape.436) | copy-start | bytes 1327108
  255.8 2.6 copy-start.6
  259.9 1.4 copy-start.3
  264.2 29.3 %all-to-all-start.7 = ((f32[1,192,3,192]{3,0,2,1:T(1,128)}), f32[1,192,3,192]{3,0,2,1:T(1,128)}, u32[]{:S(2)}, u32[]{:S(2)}) async-start(f32[1,192,3,192]{3,0,2,1:T(1,128)} %copy.289), calls=%async_computation.7 | async-start | bytes 1179648 | tf_op jit(solution)/shard_map/all_to_all | solution.py:59
  293.6 29.0 %all-to-all-start.6 = ((f32[1,192,3,192]{3,0,2,1:T(1,128)}), f32[1,192,3,192]{3,0,2,1:T(1,128)}, u32[]{:S(2)}, u32[]{:S(2)}) async-start(f32[1,192,3,192]{3,0,2,1:T(1,128)} %copy.284), calls=%async_computation.6 | async-start | bytes 1179648 | tf_op jit(solution)/shard_map/all_to_all | solution.py:58
  301.5 110.8 %all-reduce.2.cloned.1.call-start = ((), (), s32[]{:S(2)}) async-start(), calls=%async_computation.12 | async-start | bytes 1179648 | tf_op jit(solution)/shard_map/psum | solution.py:106
  330.8 1.5 copy-start.7
  412.3 3.9 copy-start.4
  421.9 34.3 %all-to-all-start.9 = ((f32[1,3,192,192]{3,0,1,2:T(1,128)}), f32[1,3,192,192]{3,0,1,2:T(1,128)}, u32[]{:S(2)}, u32[]{:S(2)}) async-start(f32[1,3,192,192]{3,0,1,2:T(1,128)} %copy.302), calls=%async_computation.9 | async-start | bytes 1179648 | tf_op jit(solution)/shard_map/all_to_all | solution.py:50
  456.2 29.4 %all-to-all-start.8 = ((f32[1,3,192,192]{3,0,1,2:T(1,128)}), f32[1,3,192,192]{3,0,1,2:T(1,128)S(1)}, u32[]{:S(2)}, u32[]{:S(2)}) async-start(f32[1,3,192,192]{3,0,1,2:T(1,128)} %copy.296), calls=%async_computation.8 | async-start | bytes 1179648 | tf_op jit(solution)/shard_map/all_to_all | solution.py:49
  486.7 1.4 copy-start.10
  489.6 1.5 copy-start.11
  496.9 29.1 %all-to-all-start.10 = ((f32[1,192,3,192]{3,0,2,1:T(1,128)}), f32[1,192,3,192]{3,0,2,1:T(1,128)}, u32[]{:S(2)}, u32[]{:S(2)}) async-start(f32[1,192,3,192]{3,0,2,1:T(1,128)} %copy.310), calls=%async_computation.10 | async-start | bytes 1179648 | tf_op jit(solution)/shard_map/all_to_all | solution.py:58
  507.6 26.0 %copy-start.12 = (f32[3,192,192]{2,1,0:T(8,128)S(1)}, f32[3,192,192]{2,1,0:T(8,128)}, u32[]{:S(2)}) copy-start(f32[3,192,192]{2,1,0:T(8,128)} %get-tuple-element.3) | copy-start | bytes 1327108
  526.0 29.0 %all-to-all-start.11 = ((f32[1,192,3,192]{3,0,2,1:T(1,128)}), f32[1,192,3,192]{3,0,2,1:T(1,128)S(1)}, u32[]{:S(2)}, u32[]{:S(2)}) async-start(f32[1,192,3,192]{3,0,2,1:T(1,128)} %copy.315), calls=%async_computation.11 | async-start | bytes 1179648 | tf_op jit(solution)/shard_map/all_to_all | solution.py:59
  555.0 0.8 copy-start.9
Sparse Core Ops, SparseCore 0:
  341.0 71.2 all-reduce.1
where the time goes:
time: 585 us; the launch traced here: 574 us
  waiting for transfers between devices  277 us (47%)
  starting transfers between devices  115 us (20%)
  matrix products  114 us (19%)
  local copies, waits for them, and re-layouts  52 us (9%)
  between operations  15.8 us (3%)
    psum x1, waiting for transfers between devices, local(): density = lax.psum(partial_value, 'band')  70 us
    all_to_all x3, waiting for transfers between devices, forward(): lax.all_to_all(real_part, 'grid', split_axis=2, concat_axis=1, tiled=True)  55.5 us
    all_to_all x3, waiting for transfers between devices, backward(): lax.all_to_all(imag_part, 'grid', split_axis=1, concat_axis=2, tiled=True)  53.7 us
    all_to_all x3, waiting for transfers between devices, backward(): lax.all_to_all(real_part, 'grid', split_axis=1, concat_axis=2, tiled=True)  50.5 us
    all_to_all x3, waiting for transfers between devices, forward(): lax.all_to_all(imag_part, 'grid', split_axis=2, concat_axis=1, tiled=True)  47.1 us
    all_to_all x3, starting transfers between devices, forward(): lax.all_to_all(imag_part, 'grid', split_axis=2, concat_axis=1, tiled=True)  41.2 us
    dot_general x18, matrix products, transform(): rc = jnp.einsum(form, real_part, cosine, precision=high)  30.9 us
    dot_general x17, matrix products, transform(): rs = jnp.einsum(form, real_part, sine, precision=high)  28.4 us
  transfers between devices with their start and end apart: 13, of which 13 were waited for; matrix products, arithmetic and copies ran while one was open for 8% of the time, Pallas kernels for 0%

commit v1 on v0

--- a/solution.py
+++ b/solution.py
@@ -1,14 +1,294 @@
+import functools
 import math
 
 import jax
 import jax.numpy as jnp
+import numpy as np
 from jax import lax
+from jax.experimental import pallas as pl
+from jax.experimental.pallas import tpu as pltpu
 from jax.sharding import PartitionSpec as P
 
 BESSEL_ZERO = 0.8462873527504802
 BESSEL_ONE = 0.36884204609417703
 BESSEL_TWO = 0.07581776248
 XC_FACTOR = 0.98474502
+MESH = pl.DeviceIdType.MESH
+N = 192
+G = 64
+SLOT = 40
+ROWS = 34
+BACK = 32
+VROWS = 7
+
+
+def circulant():
+    idx = np.arange(N)
+    freq = np.where(idx < N // 2, idx, idx - N).astype(np.float64)
+    eigen = 2.0 * freq * freq / (3.0 * (N / 2) ** 2)
+    angle = 2.0 * np.pi * ((idx[:, None] * idx[None, :]) % N) / N
+    first = (np.cos(angle) @ eigen) / N
+    return first[(idx[:, None] - idx[None, :]) % N]
+
+
+def split_table(table):
+    high = table.astype(jnp.bfloat16)
+    low = (table - high.astype(np.float64)).astype(jnp.bfloat16)
+    return np.stack([high, low])
+
+
+def halves(value):
+    high = value.astype(jnp.bfloat16)
+    return high, (value - high.astype(jnp.float32)).astype(jnp.bfloat16)
+
+
+def dot(a, b):
+    return jnp.dot(a, b, preferred_element_type=jnp.float32)
+
+
+def left_mul(table, value):
+    high, low = halves(value)
+    return dot(table[0], high) + (dot(table[0], low) + dot(table[1], high))
+
+
+def right_mul(value, table):
+    high, low = halves(value)
+    return dot(high, table[0]) + (dot(low, table[0]) + dot(high, table[1]))
+
+
+def peer(me, d):
+    yh, x, z = me // 32, (me // 8) % 4, me % 8
+    dy, dx, dz = d // 32, (d // 8) % 4, d % 8
+    return ((yh + dy) % 2) * 32 + ((x + dx) % 4) * 8 + (z + dz) % 8
+
+
+def scatter(me, src, dst, slot, rows, send_sem, recv_sem):
+    def send(s, carry):
+        to = peer(me, (s * 29) % G)
+        pltpu.make_async_remote_copy(
+            src_ref=src.at[pl.ds(pl.multiple_of(to * slot, 8), rows)],
+            dst_ref=dst.at[pl.ds(pl.multiple_of(me * slot, 8), rows)],
+            send_sem=send_sem,
+            recv_sem=recv_sem,
+            device_id={"grid": to},
+            device_id_type=MESH,
+        ).start()
+        return carry
+
+    lax.fori_loop(1, G, send, 0)
+
+
+def own(me, src, dst, slot, rows, sem):
+    return pltpu.make_async_copy(
+        src.at[pl.ds(pl.multiple_of(me * slot, 8), rows)],
+        dst.at[pl.ds(pl.multiple_of(me * slot, 8), rows)],
+        sem,
+    )
+
+
+def drain(ref, rows, sem):
+    span = ref.at[pl.ds(0, (G - 1) * rows)]
+    pltpu.make_async_copy(span, span, sem).wait()
+
+
+def propagate(
+    psi, ion, hxc, d_ref, dp_ref, fresh,
+    out_a, in_a, out_u, in_u, out_c, in_c, vshare, pot, once, twice,
+    send_sems, recv_sems, own_sems,
+):
+    me = lax.axis_index("grid")
+    core = lax.axis_index("band") % 2
+    sibling = {"band": lax.axis_index("band") + 1 - 2 * core}
+
+    barrier = pltpu.get_barrier_semaphore()
+
+    def greet(s, carry):
+        pl.semaphore_signal(barrier, inc=1, device_id={"grid": peer(me, s)}, device_id_type=MESH)
+        return carry
+
+    lax.fori_loop(1, G, greet, 0)
+    pl.semaphore_signal(barrier, inc=1, device_id=sibling, device_id_type=MESH)
+
+    blocks = []
+    tails = []
+    for x in range(3):
+        value = ion[x] + hxc[x]
+        pot[x] = value - 1.0
+        for j in range(3):
+            blocks.append(value[64 * j : 64 * j + 64, :128])
+            tails.append(value[64 * j : 64 * j + 64, 128:])
+    tails.append(tails[8])
+    for i in range(5):
+        blocks.append(jnp.concatenate([tails[2 * i], tails[2 * i + 1]], axis=1))
+    for i in range(VROWS):
+        out_a[pl.ds(27 + i, G, stride=SLOT), :] = jnp.where(core == 0, blocks[i], blocks[VROWS + i])
+    for x in range(3):
+        re, im = psi[0, x], psi[1, x]
+        kinds = (re[:, :128], im[:, :128], jnp.concatenate([re[:, 128:], im[:, 128:]], axis=1))
+        for kind in range(3):
+            for j in range(3):
+                out_a[pl.ds(x * 9 + kind * 3 + j, G, stride=SLOT), :] = kinds[kind][64 * j : 64 * j + 64]
+
+    pl.semaphore_wait(barrier, G)
+    mine = own(me, out_a, in_a, SLOT, ROWS, own_sems.at[0])
+    mine.start()
+    scatter(me, out_a, in_a, SLOT, ROWS, send_sems.at[0], recv_sems.at[0])
+
+    def inside(i, carry):
+        c, x = i // 3, i % 3
+        table = d_ref[...]
+        value = psi[c, x]
+        v = pot[x]
+        a = left_mul(table, value) + right_mul(value, table) + v * value
+        once[c, x] = a
+        twice[c, x] = left_mul(table, a) + right_mul(a, table) + v * a
+        return carry
+
+    lax.fori_loop(0, 6, inside, 0)
+
+    mine.wait()
+    drain(in_a, ROWS, recv_sems.at[0])
+
+    for i in range(VROWS):
+        vshare[core, pl.ds(64 * i, 64), :] = in_a[pl.ds(27 + i, G, stride=SLOT), :]
+    swap = pltpu.make_async_remote_copy(
+        src_ref=vshare.at[core],
+        dst_ref=vshare.at[core],
+        send_sem=send_sems.at[3],
+        recv_sem=recv_sems.at[3],
+        device_id=sibling,
+        device_id_type=MESH,
+    )
+    swap.start()
+
+    def columns(kind):
+        return jnp.concatenate(
+            [
+                jnp.concatenate(
+                    [in_a[pl.ds(x * 9 + kind * 3 + j, G, stride=SLOT), :] for j in range(3)], axis=1
+                )
+                for x in range(3)
+            ],
+            axis=0,
+        )
+
+    def spread(ref, kind, value):
+        for x in range(3):
+            for j in range(3):
+                ref[pl.ds(x * 9 + kind * 3 + j, G, stride=BACK), :] = value[
+                    64 * x : 64 * x + 64, 128 * j : 128 * j + 128
+                ]
+
+    table = dp_ref[...]
+    for kind in range(3):
+        spread(out_u, kind, left_mul(table, columns(kind)))
+    mine = own(me, out_u, in_u, BACK, 27, own_sems.at[1])
+    mine.start()
+    scatter(me, out_u, in_u, BACK, 27, send_sems.at[1], recv_sems.at[1])
+
+    swap.wait()
+
+    def vblock(i):
+        half, row = i // VROWS, i % VROWS
+        return vshare[half, 64 * row : 64 * row + 64, :]
+
+    def vtail(i):
+        pair = vblock(9 + i // 2)
+        piece = pair[:, :64] if i % 2 == 0 else pair[:, 64:]
+        return jnp.concatenate([piece, piece], axis=1)
+
+    def vcolumns(kind):
+        pick = vtail if kind == 2 else vblock
+        return jnp.concatenate(
+            [jnp.concatenate([pick(3 * x + j) for j in range(3)], axis=1) for x in range(3)], axis=0
+        )
+
+    def ucolumns(kind):
+        return jnp.concatenate(
+            [
+                jnp.concatenate(
+                    [out_u[pl.ds(x * 9 + kind * 3 + j, G, stride=BACK), :] for j in range(3)], axis=1
+                )
+                for x in range(3)
+            ],
+            axis=0,
+        )
+
+    for kind in range(3):
+        value = ucolumns(kind) + (vcolumns(kind) - 1.0) * columns(kind)
+        spread(out_c, kind, left_mul(table, value))
+    mine_c = own(me, out_c, in_c, BACK, 27, own_sems.at[2])
+    mine_c.start()
+    scatter(me, out_c, in_c, BACK, 27, send_sems.at[2], recv_sems.at[2])
+
+    def planes(ref, x):
+        kinds = [
+            jnp.concatenate(
+                [ref[pl.ds(x * 9 + kind * 3 + j, G, stride=BACK), :] for j in range(3)], axis=0
+            )
+            for kind in range(3)
+        ]
+        re = jnp.concatenate([kinds[0], kinds[2][:, :64]], axis=1)
+        im = jnp.concatenate([kinds[1], kinds[2][:, 64:]], axis=1)
+        return re, im
+
+    mine.wait()
+    drain(in_u, 27, recv_sems.at[1])
+    inner = d_ref[...]
+    alpha = BESSEL_ZERO + 2.0 * BESSEL_TWO
+    for x in range(3):
+        ure, uim = planes(in_u, x)
+        v = pot[x]
+        second_re = twice[0, x] + 2.0 * (left_mul(inner, ure) + right_mul(ure, inner)) + v * ure
+        second_im = twice[1, x] + 2.0 * (left_mul(inner, uim) + right_mul(uim, inner)) + v * uim
+        first_re = once[0, x] + ure
+        first_im = once[1, x] + uim
+        once[0, x] = alpha * psi[0, x] + 2.0 * BESSEL_ONE * first_im - 4.0 * BESSEL_TWO * second_re
+        once[1, x] = alpha * psi[1, x] - 2.0 * BESSEL_ONE * first_re - 4.0 * BESSEL_TWO * second_im
+
+    mine_c.wait()
+    drain(in_c, 27, recv_sems.at[2])
+    for x in range(3):
+        cre, cim = planes(in_c, x)
+        fresh[0, x] = once[0, x] - 4.0 * BESSEL_TWO * cre
+        fresh[1, x] = once[1, x] - 4.0 * BESSEL_TWO * cim
+
+    drain(out_a, ROWS, send_sems.at[0])
+    drain(out_u, 27, send_sems.at[1])
+    drain(out_c, 27, send_sems.at[2])
+
+
+def orbitals_step(orbitals, ion, hxc):
+    table = circulant()
+    order = np.arange(N)
+    order = 3 * (order % G) + order // G
+    vmem = pl.BlockSpec(memory_space=pltpu.VMEM)
+    f32 = jnp.float32
+    return pl.pallas_call(
+        propagate,
+        out_shape=jax.ShapeDtypeStruct((2, 3, N, N), f32),
+        in_specs=[vmem] * 5,
+        out_specs=vmem,
+        scratch_shapes=[
+            pltpu.VMEM((G * SLOT, 128), f32),
+            pltpu.VMEM((G * SLOT, 128), f32),
+            pltpu.VMEM((G * BACK, 128), f32),
+            pltpu.VMEM((G * BACK, 128), f32),
+            pltpu.VMEM((G * BACK, 128), f32),
+            pltpu.VMEM((G * BACK, 128), f32),
+            pltpu.VMEM((2, VROWS * 64, 128), f32),
+            pltpu.VMEM((3, N, N), f32),
+            pltpu.VMEM((2, 3, N, N), f32),
+            pltpu.VMEM((2, 3, N, N), f32),
+            pltpu.SemaphoreType.DMA((4,)),
+            pltpu.SemaphoreType.DMA((4,)),
+            pltpu.SemaphoreType.DMA((3,)),
+        ],
+        compiler_params=pltpu.CompilerParams(
+            collective_id=1, has_side_effects=True, vmem_limit_bytes=56 << 20
+        ),
+        name="propagate",
+    )(orbitals, ion, hxc, split_table(table), split_table(table[order][:, order]))
 
 
 def tables(length):
@@ -83,23 +363,9 @@
     columns = length // lax.axis_size("grid")
     grid_pos = lax.axis_index("grid")
     squares = squares_block(length, grid_pos * columns, columns, length)
-    kinetic = 2.0 * squares / (3.0 * (length / 2) ** 2) - 1.0
-    potential = ion_potential + hxc_potential
-
-    def hamilton(real_part, imag_part):
-        fre, fim = forward(real_part, imag_part)
-        back_re, back_im = backward(kinetic * fre, kinetic * fim)
-        return (back_re + potential * real_part, back_im + potential * imag_part)
-
-    psi_re = orbitals[:, 0]
-    psi_im = orbitals[:, 1]
-    first_re, first_im = hamilton(psi_re, psi_im)
-    again_re, again_im = hamilton(first_re, first_im)
-    second_re = 2.0 * again_re - psi_re
-    second_im = 2.0 * again_im - psi_im
-    fresh_re = BESSEL_ZERO * psi_re + 2.0 * BESSEL_ONE * first_im - 2.0 * BESSEL_TWO * second_re
-    fresh_im = BESSEL_ZERO * psi_im - 2.0 * BESSEL_ONE * first_re - 2.0 * BESSEL_TWO * second_im
-    new_orbitals = jnp.stack([fresh_re, fresh_im], axis=1)
+    fresh = orbitals_step(orbitals[0], ion_potential, hxc_potential)
+    fresh_re, fresh_im = fresh[None, 0], fresh[None, 1]
+    new_orbitals = fresh[None]
     partial_value = jnp.sum(
         occupations[:, None, None, None] * (fresh_re * fresh_re + fresh_im * fresh_im), axis=0
     )

time: 585 us -> 342 us (0.58)
  the two profiles are of different devices: /device:TPU:6 before, /device:TPU:1 now
where the time goes in v1:
time: 342 us; the launch traced here: 337 us
  waiting for transfers between devices  139 us (41%)
  Pallas kernels  90.7 us (27%)
  starting transfers between devices  46.2 us (14%)
  matrix products  33.6 us (10%)
  between operations  15.4 us (5%)
  local copies, waits for them, and re-layouts  9.93 us (3%)
    pallas_call x1, Pallas kernels, orbitals_step(): pl.pallas_call(propagate, out_shape=jax.ShapeDtypeStruct((2, 3, N, N), f3...  90.7 us
    psum x1, waiting for transfers between devices, local(): density = lax.psum(partial_value, 'band')  74.4 us
    all_to_all x1, waiting for transfers between devices, backward(): lax.all_to_all(real_part, 'grid', split_axis=1, concat_axis=2, tiled=True)  18.7 us
    all_to_all x1, waiting for transfers between devices, forward(): lax.all_to_all(imag_part, 'grid', split_axis=2, concat_axis=1, tiled=True)  17.8 us
    all_to_all x1, waiting for transfers between devices, backward(): lax.all_to_all(imag_part, 'grid', split_axis=1, concat_axis=2, tiled=True)  14.8 us
    all_to_all x1, starting transfers between devices, forward(): lax.all_to_all(real_part, 'grid', split_axis=2, concat_axis=1, tiled=True)  14.4 us
    all_to_all x1, waiting for transfers between devices, forward(): lax.all_to_all(real_part, 'grid', split_axis=2, concat_axis=1, tiled=True)  13 us
    all_to_all x1, starting transfers between devices, forward(): lax.all_to_all(imag_part, 'grid', split_axis=2, concat_axis=1, tiled=True)  11.8 us
  transfers between devices with their start and end apart: 5, of which 5 were waited for; matrix products, arithmetic and copies ran while one was open for 3% of the time, Pallas kernels for 0%

profile of v1, /device:TPU:1, one launch (start us, length us, event | category | flops | bytes accessed | tf_op | source)
XLA Modules:
  0.0 336.8 jit_solution(17147134693892208106)
XLA Ops:
  7.9 90.7 %propagate.1 = f32[2,3,192,192]{3,2,1,0:T(8,128)} custom-call(f32[2,3,192,192]{3,2,1,0:T(8,128)} %bitcast.133, f32[3,192,192]{2,1,0:T(8,128)} %ion.1, f32[3,192,192]{2,1,0:T(8,128)} %hxc.1, bf16[2,192,192]{2,1,0:T(8,128)(2,1)} %constant.60.clone.d_ref, bf16[2,192,192]{2,1,0:T(8,128)(2,1)} %constant.61.clone.dp_ref), custom_call_target="tpu_custom_call" | custom-call | tf_op jit(solution)/shard_map/propagate/pallas_call | solution.py:267
  98.6 2.1 multiply_bitcast_fusion
  102.2 74.4 %all-reduce.2.cloned.1.call-done = f32[3,192,192]{2,1,0:T(8,128)} async-done(((f32[3,192,192]{2,1,0:T(8,128)}), f32[3,192,192]{2,1,0:T(8,128)}) %all-reduce.2.cloned.1.call-update) | async-done | bytes 442384 | tf_op jit(solution)/shard_map/psum | solution.py:372
  176.5 2.4 fusion.43
  180.4 1.4 fusion.45
  183.2 1.4 fusion.13
  184.7 1.4 copy.78
  186.1 14.4 %all-to-all-start = ((f32[1,3,192,192]{3,0,1,2:T(1,128)}), f32[1,3,192,192]{3,0,1,2:T(1,128)S(1)}, u32[]{:S(2)}, u32[]{:S(2)}) async-start(f32[1,3,192,192]{3,0,1,2:T(1,128)} %copy.78), calls=%async_computation | async-start | bytes 1179648 | tf_op jit(solution)/shard_map/all_to_all | solution.py:329
  200.5 1.4 fusion.38
  202.0 1.4 fusion.12
  203.4 1.4 copy.84
  204.8 13.0 %all-to-all-done = f32[1,3,192,192]{3,0,1,2:T(1,128)S(1)} async-done(((f32[1,3,192,192]{3,0,1,2:T(1,128)}), f32[1,3,192,192]{3,0,1,2:T(1,128)S(1)}, u32[]{:S(2)}, u32[]{:S(2)}) %all-to-all-start) | async-done | bytes 442400 | tf_op jit(solution)/shard_map/all_to_all | solution.py:329
  217.9 11.8 %all-to-all-start.1 = ((f32[1,3,192,192]{3,0,1,2:T(1,128)}), f32[1,3,192,192]{3,0,1,2:T(1,128)S(1)}, u32[]{:S(2)}, u32[]{:S(2)}) async-start(f32[1,3,192,192]{3,0,1,2:T(1,128)} %copy.84), calls=%async_computation.1 | async-start | bytes 1179648 | tf_op jit(solution)/shard_map/all_to_all | solution.py:330
  230.9 17.8 %all-to-all-done.1 = f32[1,3,192,192]{3,0,1,2:T(1,128)S(1)} async-done(((f32[1,3,192,192]{3,0,1,2:T(1,128)}), f32[1,3,192,192]{3,0,1,2:T(1,128)S(1)}, u32[]{:S(2)}, u32[]{:S(2)}) %all-to-all-start.1) | async-done | bytes 442400 | tf_op jit(solution)/shard_map/all_to_all | solution.py:330
  251.2 1.4 fusion.47
  252.7 1.5 fusion.10
  254.2 1.5 fusion.11
  255.7 1.4 fusion.34
  257.1 1.4 fusion.7
  258.5 1.4 copy.97
  260.0 10.1 %all-to-all-start.3 = ((f32[1,192,3,192]{3,0,2,1:T(1,128)}), f32[1,192,3,192]{3,0,2,1:T(1,128)S(1)}, u32[]{:S(2)}, u32[]{:S(2)}) async-start(f32[1,192,3,192]{3,0,2,1:T(1,128)} %copy.97), calls=%async_computation.3 | async-start | bytes 1179648 | tf_op jit(solution)/shard_map/all_to_all | solution.py:339
  270.1 1.4 fusion.49
  271.5 1.4 fusion.9
  273.0 1.4 copy.92
  274.4 14.8 %all-to-all-done.3 = f32[1,192,3,192]{3,0,2,1:T(1,128)S(1)} async-done(((f32[1,192,3,192]{3,0,2,1:T(1,128)}), f32[1,192,3,192]{3,0,2,1:T(1,128)S(1)}, u32[]{:S(2)}, u32[]{:S(2)}) %all-to-all-start.3) | async-done | bytes 442400 | tf_op jit(solution)/shard_map/all_to_all | solution.py:339
  289.2 9.8 %all-to-all-start.2 = ((f32[1,192,3,192]{3,0,2,1:T(1,128)}), f32[1,192,3,192]{3,0,2,1:T(1,128)S(1)}, u32[]{:S(2)}, u32[]{:S(2)}) async-start(f32[1,192,3,192]{3,0,2,1:T(1,128)} %copy.92), calls=%async_computation.2 | async-start | bytes 1179648 | tf_op jit(solution)/shard_map/all_to_all | solution.py:338
  299.5 18.7 %all-to-all-done.2 = f32[1,192,3,192]{3,0,2,1:T(1,128)S(1)} async-done(((f32[1,192,3,192]{3,0,2,1:T(1,128)}), f32[1,192,3,192]{3,0,2,1:T(1,128)S(1)}, u32[]{:S(2)}, u32[]{:S(2)}) %all-to-all-start.2) | async-done | bytes 442400 | tf_op jit(solution)/shard_map/all_to_all | solution.py:338
  318.7 1.4 fusion.51
  320.1 1.4 fusion.32
  321.6 1.4 fusion.5
  323.0 1.4 fusion.3
  325.9 2.6 fusion.1
  (25 shorter events, 11.3 us)
Async XLA Ops:
  7.2 169.4 %all-reduce.2.cloned.1.call-start = ((), (), s32[]{:S(2)}) async-start(), calls=%async_computation.4 | async-start | bytes 1179648 | tf_op jit(solution)/shard_map/psum | solution.py:372
  179.0 2.8 copy-start.1
  186.1 31.8 %all-to-all-start = ((f32[1,3,192,192]{3,0,1,2:T(1,128)}), f32[1,3,192,192]{3,0,1,2:T(1,128)S(1)}, u32[]{:S(2)}, u32[]{:S(2)}) async-start(f32[1,3,192,192]{3,0,1,2:T(1,128)} %copy.78), calls=%async_computation | async-start | bytes 1179648 | tf_op jit(solution)/shard_map/all_to_all | solution.py:329
  217.9 30.8 %all-to-all-start.1 = ((f32[1,3,192,192]{3,0,1,2:T(1,128)}), f32[1,3,192,192]{3,0,1,2:T(1,128)S(1)}, u32[]{:S(2)}, u32[]{:S(2)}) async-start(f32[1,3,192,192]{3,0,1,2:T(1,128)} %copy.84), calls=%async_computation.1 | async-start | bytes 1179648 | tf_op jit(solution)/shard_map/all_to_all | solution.py:330
  260.0 29.2 %all-to-all-start.3 = ((f32[1,192,3,192]{3,0,2,1:T(1,128)}), f32[1,192,3,192]{3,0,2,1:T(1,128)S(1)}, u32[]{:S(2)}, u32[]{:S(2)}) async-start(f32[1,192,3,192]{3,0,2,1:T(1,128)} %copy.97), calls=%async_computation.3 | async-start | bytes 1179648 | tf_op jit(solution)/shard_map/all_to_all | solution.py:339
  289.2 29.0 %all-to-all-start.2 = ((f32[1,192,3,192]{3,0,2,1:T(1,128)}), f32[1,192,3,192]{3,0,2,1:T(1,128)S(1)}, u32[]{:S(2)}, u32[]{:S(2)}) async-start(f32[1,192,3,192]{3,0,2,1:T(1,128)} %copy.92), calls=%async_computation.2 | async-start | bytes 1179648 | tf_op jit(solution)/shard_map/all_to_all | solution.py:338
  325.9 2.6 copy-start
Sparse Core Ops, SparseCore 0:
  100.9 75.5 all-reduce.1

commit v2 on v1

--- a/solution.py
+++ b/solution.py
@@ -1,4 +1,3 @@
-import functools
 import math
 
 import jax
@@ -20,6 +19,9 @@
 ROWS = 34
 BACK = 32
 VROWS = 7
+SHARE = 40
+UNIT = 3 * SHARE
+HALF = 4 * UNIT
 
 
 def circulant():
@@ -31,10 +33,19 @@
     return first[(idx[:, None] - idx[None, :]) % N]
 
 
-def split_table(table):
-    high = table.astype(jnp.bfloat16)
-    low = (table - high.astype(np.float64)).astype(jnp.bfloat16)
-    return np.stack([high, low])
+def hartley():
+    idx = np.arange(N)
+    angle = 2.0 * np.pi * ((idx[:, None] * idx[None, :]) % N) / N
+    return (np.cos(angle) + np.sin(angle)) / math.sqrt(N)
+
+
+def split_table(table, parts=2):
+    pieces = []
+    for _ in range(parts):
+        piece = table.astype(jnp.bfloat16)
+        pieces.append(piece)
+        table = table - piece.astype(np.float64)
+    return np.stack(pieces)
 
 
 def halves(value):
@@ -54,6 +65,36 @@
 def right_mul(value, table):
     high, low = halves(value)
     return dot(high, table[0]) + (dot(low, table[0]) + dot(high, table[1]))
+
+
+def thirds(value):
+    high, rest = halves(value)
+    left = value - high.astype(jnp.float32)
+    return high, rest, (left - rest.astype(jnp.float32)).astype(jnp.bfloat16)
+
+
+def left_fine(table, value):
+    high, mid, low = thirds(value)
+    small = dot(table[2], high) + dot(table[1], mid) + dot(table[0], low)
+    return dot(table[0], high) + (dot(table[1], high) + dot(table[0], mid) + small)
+
+
+def right_fine(value, table):
+    high, mid, low = thirds(value)
+    small = dot(high, table[2]) + dot(mid, table[1]) + dot(low, table[0])
+    return dot(high, table[0]) + (dot(high, table[1]) + dot(mid, table[0]) + small)
+
+
+def frequency(idx):
+    return jnp.where(idx < N // 2, idx, idx - N).astype(jnp.float32)
+
+
+def row_of(device):
+    return (device * 9 + 15) // 16
+
+
+def holds_row(device):
+    return (row_of(device) * 16) // 9 == device
 
 
 def peer(me, d):
@@ -92,13 +133,18 @@
 
 
 def propagate(
-    psi, ion, hxc, d_ref, dp_ref, fresh,
+    psi, occ, ion, hxc, d_ref, dp_ref, h_ref, hx_ref, hxt_ref, fresh, new_pot,
     out_a, in_a, out_u, in_u, out_c, in_c, vshare, pot, once, twice,
-    send_sems, recv_sems, own_sems,
+    pairs, part_s, part_r, core_s, core_r, runs_s, runs_r, from_s, from_r,
+    to_rows, at_rows, back_rows, got_rows, all_s, all_r,
+    send_sems, recv_sems, own_sems, band_send, band_recv,
 ):
     me = lax.axis_index("grid")
-    core = lax.axis_index("band") % 2
-    sibling = {"band": lax.axis_index("band") + 1 - 2 * core}
+    band = lax.axis_index("band")
+    core = band % 2
+    line = band // 2
+    sibling = {"band": band + 1 - 2 * core}
+    others = [(line + d) % 4 for d in range(1, 4)]
 
     barrier = pltpu.get_barrier_semaphore()
 
@@ -108,6 +154,10 @@
 
     lax.fori_loop(1, G, greet, 0)
     pl.semaphore_signal(barrier, inc=1, device_id=sibling, device_id_type=MESH)
+    for other in others:
+        pl.semaphore_signal(
+            barrier, inc=1, device_id={"band": 2 * other + core}, device_id_type=MESH
+        )
 
     blocks = []
     tails = []
@@ -129,7 +179,7 @@
             for j in range(3):
                 out_a[pl.ds(x * 9 + kind * 3 + j, G, stride=SLOT), :] = kinds[kind][64 * j : 64 * j + 64]
 
-    pl.semaphore_wait(barrier, G)
+    pl.semaphore_wait(barrier, G + 3)
     mine = own(me, out_a, in_a, SLOT, ROWS, own_sems.at[0])
     mine.start()
     scatter(me, out_a, in_a, SLOT, ROWS, send_sems.at[0], recv_sems.at[0])
@@ -248,133 +298,287 @@
 
     mine_c.wait()
     drain(in_c, 27, recv_sems.at[2])
+    table_h = h_ref[...]
+    weight = occ[0]
+
+    def pack(ref, x, value):
+        pairs[...] = jnp.concatenate([value[:96, 128:], value[96:, 128:]], axis=1)
+        for b in range(8):
+            base = (((b % 2) * 4 + b // 2) * 3 + x) * SHARE
+            ref[base : base + 24, :] = value[24 * b : 24 * b + 24, :128]
+            ref[base + 24 : base + 36, :] = pairs[12 * b : 12 * b + 12, :]
+            ref[base + 36 : base + 40, :] = jnp.zeros((4, 128), jnp.float32)
+
     for x in range(3):
         cre, cim = planes(in_c, x)
-        fresh[0, x] = once[0, x] - 4.0 * BESSEL_TWO * cre
-        fresh[1, x] = once[1, x] - 4.0 * BESSEL_TWO * cim
+        re = once[0, x] - 4.0 * BESSEL_TWO * cre
+        im = once[1, x] - 4.0 * BESSEL_TWO * cim
+        fresh[0, x] = re
+        fresh[1, x] = im
+        rho = weight * (re * re + im * im)
+        pack(part_r, x, rho)
+        pack(part_s, x, right_fine(left_fine(table_h, rho), table_h))
+
+    def swap_half(src, dst, k):
+        half = pl.multiple_of((1 - core) * HALF, 8)
+        copy = pltpu.make_async_remote_copy(
+            src_ref=src.at[pl.ds(half, HALF)],
+            dst_ref=dst,
+            send_sem=band_send.at[k],
+            recv_sem=band_recv.at[k],
+            device_id=sibling,
+            device_id_type=MESH,
+        )
+        copy.start()
+        return copy
+
+    def add_half(src, dst, out):
+        out[...] = src[pl.ds(pl.multiple_of(core * HALF, 8), HALF), :] + dst[...]
+
+    def to_lines(src, dst, k):
+        copies = []
+        for i, other in enumerate(others):
+            copy = pltpu.make_async_remote_copy(
+                src_ref=src.at[pl.ds(pl.multiple_of(other * UNIT, 8), UNIT)],
+                dst_ref=dst.at[pl.ds(pl.multiple_of(line * UNIT, 8), UNIT)],
+                send_sem=band_send.at[k + i],
+                recv_sem=band_recv.at[k + i],
+                device_id={"band": 2 * other + core},
+                device_id_type=MESH,
+            )
+            copy.start()
+            copies.append(copy)
+        mine = pl.ds(pl.multiple_of(line * UNIT, 8), UNIT)
+        dst[mine, :] = src[mine, :]
+        return copies
+
+    def total(ref):
+        return (ref[0:UNIT, :] + ref[UNIT : 2 * UNIT, :]) + (
+            ref[2 * UNIT : 3 * UNIT, :] + ref[3 * UNIT : 4 * UNIT, :]
+        )
+
+    swap_s = swap_half(part_s, core_s, 0)
+    swap_r = swap_half(part_r, core_r, 1)
+    swap_s.wait()
+    add_half(part_s, core_s, runs_s)
+    lines_s = to_lines(runs_s, from_s, 2)
+    swap_r.wait()
+    add_half(part_r, core_r, runs_r)
+    lines_r = to_lines(runs_r, from_r, 5)
+    for copy in lines_s:
+        copy.wait()
+
+    share = total(from_s)
+    for x in range(3):
+        to_rows[pl.ds(x, SHARE, stride=8), :] = share[SHARE * x : SHARE * x + SHARE]
+    row = row_of(me)
+    holder = holds_row(me)
+
+    def send_row(s, carry):
+        to = peer(me, (s * 29) % G)
+
+        @pl.when(holds_row(to))
+        def _():
+            pltpu.make_async_remote_copy(
+                src_ref=to_rows.at[pl.ds(pl.multiple_of(row_of(to) * 8, 8), 3)],
+                dst_ref=at_rows.at[pl.ds(pl.multiple_of(me * 8, 8), 3)],
+                send_sem=send_sems.at[4],
+                recv_sem=recv_sems.at[4],
+                device_id={"grid": to},
+                device_id_type=MESH,
+            ).start()
+
+        return carry
+
+    lax.fori_loop(1, G, send_row, 0)
+
+    for copy in lines_r:
+        copy.wait()
+
+    def gather_start(ref, k):
+        mine = ref.at[pl.ds(pl.multiple_of(core * HALF + line * UNIT, 8), UNIT)]
+        copies = []
+        for i, other in enumerate(others):
+            copy = pltpu.make_async_remote_copy(
+                src_ref=mine,
+                dst_ref=mine,
+                send_sem=band_send.at[k + i],
+                recv_sem=band_recv.at[k + i],
+                device_id={"band": 2 * other + core},
+                device_id_type=MESH,
+            )
+            copy.start()
+            copies.append(copy)
+        return copies
+
+    def gather_cores(ref, k):
+        half = ref.at[pl.ds(pl.multiple_of(core * HALF, 8), HALF)]
+        copy = pltpu.make_async_remote_copy(
+            src_ref=half,
+            dst_ref=half,
+            send_sem=band_send.at[k],
+            recv_sem=band_recv.at[k],
+            device_id=sibling,
+            device_id_type=MESH,
+        )
+        copy.start()
+        return copy
+
+    place = pl.ds(pl.multiple_of(core * HALF + line * UNIT, 8), UNIT)
+    rho_share = total(from_r)
+    root = jnp.exp(jnp.log(jnp.maximum(rho_share, 1e-37)) * (1.0 / 3.0))
+    all_r[place, :] = -XC_FACTOR * jnp.where(rho_share > 0, root, 0.0)
+    gather_r = gather_start(all_r, 8)
+
+    @pl.when(holder)
+    def _():
+        at_rows[pl.ds(pl.multiple_of(me * 8, 8), 8), :] = to_rows[
+            pl.ds(pl.multiple_of(row * 8, 8), 8), :
+        ]
+        drain(at_rows, 3, recv_sems.at[4])
+        lines = jnp.concatenate([at_rows[pl.ds(x, G, stride=8), :] for x in range(3)], axis=0)
+        spectrum = left_fine(hx_ref[...], lines)
+        kx = lax.broadcasted_iota(jnp.int32, (N, 128), 0)
+        lane = lax.broadcasted_iota(jnp.int32, (N, 128), 1)
+        pair = 12 * band + row - 24
+        wide = row < 24
+        right = lane >= 64
+        ky = jnp.where(wide, 24 * band + row, jnp.where(right, pair + 96, pair))
+        kz = jnp.where(wide, lane, jnp.where(right, lane + 64, lane + 128))
+        fx, fy, fz = frequency(kx), frequency(ky), frequency(kz)
+        kk = fx * fx + fy * fy + fz * fz
+        kernel = jnp.where(kk > 0, (N * math.sqrt(N) / 16.0) / (kk + 1.0), 0.0)
+        result = left_mul(hxt_ref[...], kernel * spectrum)
+        for x in range(3):
+            back_rows[pl.ds(x, G, stride=8), :] = result[64 * x : 64 * x + 64]
+
+        def send_back(s, carry):
+            to = peer(me, (s * 29) % G)
+            pltpu.make_async_remote_copy(
+                src_ref=back_rows.at[pl.ds(pl.multiple_of(to * 8, 8), 3)],
+                dst_ref=got_rows.at[pl.ds(pl.multiple_of(row * 8, 8), 3)],
+                send_sem=send_sems.at[5],
+                recv_sem=recv_sems.at[5],
+                device_id={"grid": to},
+                device_id_type=MESH,
+            ).start()
+            return carry
+
+        lax.fori_loop(1, G, send_back, 0)
+        got_rows[pl.ds(pl.multiple_of(row * 8, 8), 8), :] = back_rows[
+            pl.ds(pl.multiple_of(me * 8, 8), 8), :
+        ]
+
+    def drain_rows(sem):
+        @pl.when(holder)
+        def _():
+            span = to_rows.at[pl.ds(0, 35 * 3)]
+            pltpu.make_async_copy(span, span, sem).wait()
+
+        @pl.when(jnp.logical_not(holder))
+        def _():
+            span = to_rows.at[pl.ds(0, 36 * 3)]
+            pltpu.make_async_copy(span, span, sem).wait()
+
+    for copy in gather_r:
+        copy.wait()
+    cores_r = gather_cores(all_r, 11)
+
+    drain_rows(recv_sems.at[5])
+    for x in range(3):
+        all_s[pl.ds(pl.multiple_of(core * HALF + line * UNIT + SHARE * x, 8), SHARE), :] = got_rows[
+            pl.ds(x, SHARE, stride=8), :
+        ]
+    for copy in gather_start(all_s, 12):
+        copy.wait()
+    cores_r.wait()
+    gather_cores(all_s, 15).wait()
+
+    def unpack(ref, x):
+        wide = []
+        for b in range(8):
+            base = (((b % 2) * 4 + b // 2) * 3 + x) * SHARE
+            wide.append(ref[base : base + 24, :])
+            pairs[12 * b : 12 * b + 12, :] = ref[base + 24 : base + 36, :]
+        tail = pairs[...]
+        tail = jnp.concatenate([tail[:, :64], tail[:, 64:]], axis=0)
+        return jnp.concatenate([jnp.concatenate(wide, axis=0), tail], axis=1)
+
+    for x in range(3):
+        spectrum = unpack(all_s, x)
+        new_pot[x] = right_mul(left_mul(table_h, spectrum), table_h) + unpack(all_r, x)
 
     drain(out_a, ROWS, send_sems.at[0])
     drain(out_u, 27, send_sems.at[1])
     drain(out_c, 27, send_sems.at[2])
-
-
-def orbitals_step(orbitals, ion, hxc):
+    drain_rows(send_sems.at[4])
+
+    @pl.when(holder)
+    def _():
+        drain(back_rows, 3, send_sems.at[5])
+
+
+def local(orbitals, occupations, ion, hxc):
     table = circulant()
+    cas = hartley()
     order = np.arange(N)
     order = 3 * (order % G) + order // G
     vmem = pl.BlockSpec(memory_space=pltpu.VMEM)
     f32 = jnp.float32
-    return pl.pallas_call(
+    slots = lambda rows: pltpu.VMEM((rows, 128), f32)
+    fresh, new_pot = pl.pallas_call(
         propagate,
-        out_shape=jax.ShapeDtypeStruct((2, 3, N, N), f32),
-        in_specs=[vmem] * 5,
-        out_specs=vmem,
+        out_shape=(jax.ShapeDtypeStruct((2, 3, N, N), f32), jax.ShapeDtypeStruct((3, N, N), f32)),
+        in_specs=[vmem, pl.BlockSpec(memory_space=pltpu.SMEM)] + [vmem] * 7,
+        out_specs=(vmem, vmem),
         scratch_shapes=[
-            pltpu.VMEM((G * SLOT, 128), f32),
-            pltpu.VMEM((G * SLOT, 128), f32),
-            pltpu.VMEM((G * BACK, 128), f32),
-            pltpu.VMEM((G * BACK, 128), f32),
-            pltpu.VMEM((G * BACK, 128), f32),
-            pltpu.VMEM((G * BACK, 128), f32),
+            slots(G * SLOT),
+            slots(G * SLOT),
+            slots(G * BACK),
+            slots(G * BACK),
+            slots(G * BACK),
+            slots(G * BACK),
             pltpu.VMEM((2, VROWS * 64, 128), f32),
             pltpu.VMEM((3, N, N), f32),
             pltpu.VMEM((2, 3, N, N), f32),
             pltpu.VMEM((2, 3, N, N), f32),
-            pltpu.SemaphoreType.DMA((4,)),
-            pltpu.SemaphoreType.DMA((4,)),
+            slots(96),
+            slots(2 * HALF),
+            slots(2 * HALF),
+            slots(HALF),
+            slots(HALF),
+            slots(HALF),
+            slots(HALF),
+            slots(HALF),
+            slots(HALF),
+            slots(SHARE * 8),
+            slots(G * 8),
+            slots(G * 8),
+            slots(SHARE * 8),
+            slots(2 * HALF),
+            slots(2 * HALF),
+            pltpu.SemaphoreType.DMA((6,)),
+            pltpu.SemaphoreType.DMA((6,)),
             pltpu.SemaphoreType.DMA((3,)),
+            pltpu.SemaphoreType.DMA((16,)),
+            pltpu.SemaphoreType.DMA((16,)),
         ],
         compiler_params=pltpu.CompilerParams(
             collective_id=1, has_side_effects=True, vmem_limit_bytes=56 << 20
         ),
         name="propagate",
-    )(orbitals, ion, hxc, split_table(table), split_table(table[order][:, order]))
-
-
-def tables(length):
-    idx = jnp.arange(length, dtype=jnp.int32)
-    angle = (idx[:, None] * idx[None, :] % length).astype(jnp.float32) * (2.0 * math.pi / length)
-    return (jnp.cos(angle), jnp.sin(angle))
-
-
-def transform(real_part, imag_part, form, inverse, length):
-    cosine, sine = tables(length)
-    high = lax.Precision.HIGHEST
-    rc = jnp.einsum(form, real_part, cosine, precision=high)
-    rs = jnp.einsum(form, real_part, sine, precision=high)
-    ic = jnp.einsum(form, imag_part, cosine, precision=high)
-    isn = jnp.einsum(form, imag_part, sine, precision=high)
-    if inverse:
-        scale = 1.0 / length
-        return ((rc - isn) * scale, (ic + rs) * scale)
-    return (rc + isn, ic - rs)
-
-
-def along_z(real_part, imag_part, inverse):
-    return transform(real_part, imag_part, "oxyn,nk->oxyk", inverse, real_part.shape[3])
-
-
-def along_y(real_part, imag_part, inverse):
-    return transform(real_part, imag_part, "oxnz,nk->oxkz", inverse, real_part.shape[2])
-
-
-def along_x(real_part, imag_part, inverse):
-    return transform(real_part, imag_part, "onyz,nk->okyz", inverse, real_part.shape[1])
-
-
-def forward(real_part, imag_part):
-    real_part, imag_part = along_z(real_part, imag_part, False)
-    real_part, imag_part = along_y(real_part, imag_part, False)
-    real_part, imag_part = (
-        lax.all_to_all(real_part, "grid", split_axis=2, concat_axis=1, tiled=True),
-        lax.all_to_all(imag_part, "grid", split_axis=2, concat_axis=1, tiled=True),
+    )(
+        orbitals[0],
+        occupations,
+        ion,
+        hxc,
+        split_table(table),
+        split_table(table[order][:, order]),
+        split_table(cas, 3),
+        split_table(cas[:, order], 3),
+        split_table(cas[:, order].T),
     )
-    return along_x(real_part, imag_part, False)
-
-
-def backward(real_part, imag_part):
-    real_part, imag_part = along_x(real_part, imag_part, True)
-    real_part, imag_part = (
-        lax.all_to_all(real_part, "grid", split_axis=1, concat_axis=2, tiled=True),
-        lax.all_to_all(imag_part, "grid", split_axis=1, concat_axis=2, tiled=True),
-    )
-    real_part, imag_part = along_y(real_part, imag_part, True)
-    real_part, imag_part = along_z(real_part, imag_part, True)
-    return (real_part, imag_part)
-
-
-def frequency(idx, length):
-    return jnp.where(idx < length // 2, idx, idx - length).astype(jnp.float32)
-
-
-def squares_block(x_count, y_start, y_count, length):
-    fx = frequency(jnp.arange(x_count, dtype=jnp.int32), length)
-    fy = frequency(y_start + jnp.arange(y_count, dtype=jnp.int32), length)
-    fz = frequency(jnp.arange(length, dtype=jnp.int32), length)
-    return (fx * fx)[:, None, None] + (fy * fy)[None, :, None] + (fz * fz)[None, None, :]
-
-
-def hartree_filter(squares, length):
-    return jnp.where(squares > 0, length * math.sqrt(length) / 16.0 / (squares + 1.0), 0.0)
-
-
-def local(orbitals, occupations, ion_potential, hxc_potential):
-    length = orbitals.shape[-1]
-    columns = length // lax.axis_size("grid")
-    grid_pos = lax.axis_index("grid")
-    squares = squares_block(length, grid_pos * columns, columns, length)
-    fresh = orbitals_step(orbitals[0], ion_potential, hxc_potential)
-    fresh_re, fresh_im = fresh[None, 0], fresh[None, 1]
-    new_orbitals = fresh[None]
-    partial_value = jnp.sum(
-        occupations[:, None, None, None] * (fresh_re * fresh_re + fresh_im * fresh_im), axis=0
-    )
-    density = lax.psum(partial_value, "band")
-    fre, fim = forward(density[None], jnp.zeros_like(density)[None])
-    kernel = hartree_filter(squares, length)
-    hart_re, hart_im = backward(kernel * fre, kernel * fim)
-    new_potential = hart_re[0] - XC_FACTOR * jnp.cbrt(density)
-    return (new_orbitals, new_potential)
+    return fresh[None], new_pot
 
 
 def solution(mesh):

time: 342 us -> 144 us (0.42); the launches traced: 337 us -> 143 us
  waiting for transfers between devices: 139 us -> 0 us
  Pallas kernels: 90.7 us -> 139 us
  starting transfers between devices: 46.2 us -> 0 us
  matrix products: 33.6 us -> 0 us
  between operations: 15.4 us -> 1.29 us
  local copies, waits for them, and re-layouts: 9.93 us -> 3.3 us
    psum x1 -> x0, waiting for transfers between devices: 74.4 us -> none  [local(): density = lax.psum(partial_value, 'band')]
    all_to_all x4 -> x0, waiting for transfers between devices: 64.3 us -> none  [the longest x1 18.7 us: backward(): lax.all_to_all(real_part, 'grid', split_axis=1, concat_axis=2, tiled=True)]
    pallas_call x1, Pallas kernels: 90.7 us -> 139 us  [local(): pl.pallas_call(propagate, out_shape=(jax.ShapeDtypeStruct((2, 3, N, N), f...]
    all_to_all x4 -> x0, starting transfers between devices: 46.1 us -> none  [the longest x1 14.4 us: forward(): lax.all_to_all(real_part, 'grid', split_axis=2, concat_axis=1, tiled=True)]
    dot_general x22 -> x0, matrix products: 33.6 us -> none  [the longest x6 9.8 us: transform(): isn = jnp.einsum(form, imag_part, sine, precision=high)]
  transfers between devices with their start and end apart: 5 -> 0, of which waited for: 5 -> 0; matrix products, arithmetic and copies ran while one was open for 3% -> 0% of each run, Pallas kernels for 0% -> 0%
where the time goes in v2:
time: 144 us; the launch traced here: 143 us
  Pallas kernels  139 us (97%)
  local copies, waits for them, and re-layouts  3.3 us (2%)
    pallas_call x1, Pallas kernels, local(): pl.pallas_call(propagate, out_shape=(jax.ShapeDtypeStruct((2, 3, N, N), f...  139 us
    unnamed x4, local copies, waits for them, and re-layouts  3.3 us

profile of v2, /device:TPU:1, one launch (start us, length us, event | category | flops | bytes accessed | tf_op | source)
XLA Modules:
  0.0 143.3 jit_solution(7735189127315088199)
XLA Ops:
  1.3 138.8 %propagate.1 = (f32[2,3,192,192]{3,2,1,0:T(8,128)}, f32[3,192,192]{2,1,0:T(8,128)}) custom-call(f32[2,3,192,192]{3,2,1,0:T(8,128)} %bitcast.3, f32[1]{0:T(128)S(6)} %copy.13.occ, f32[3,192,192]{2,1,0:T(8,128)} %ion.1, f32[3,192,192]{2,1,0:T(8,128)} %hxc.1, bf16[2,192,192]{2,1,0:T(8,128)(2,1)} %constant.10.clone.d_ref, ...), custom_call_target="tpu_custom_call" | custom-call | tf_op jit(solution)/shard_map/propagate/pallas_call | solution.py:529
  140.0 0.0 copy-start
  140.0 2.5 %copy.14 = f32[1,2,3,192,192]{4,3,2,1,0:T(8,128)} copy(f32[1,2,3,192,192]{4,3,2,1,0:T(8,128)} %bitcast.2) | data formatting | bytes 1769472
  142.5 0.0 copy-done
  142.5 0.8 copy.15
Async XLA Ops:
  140.0 2.5 %copy-start = (f32[3,192,192]{2,1,0:T(8,128)S(1)}, f32[3,192,192]{2,1,0:T(8,128)}, u32[]{:S(2)}) copy-start(f32[3,192,192]{2,1,0:T(8,128)} %get-tuple-element.9) | copy-start | bytes 1327108

commit v3 on v2

--- a/solution.py
+++ b/solution.py
@@ -16,8 +16,8 @@
 N = 192
 G = 64
 SLOT = 40
-ROWS = 34
-BACK = 32
+WIDE = 18
+TAIL = 24
 VROWS = 7
 SHARE = 40
 UNIT = 3 * SHARE
@@ -89,42 +89,50 @@
     return jnp.where(idx < N // 2, idx, idx - N).astype(jnp.float32)
 
 
-def row_of(device):
-    return (device * 9 + 15) // 16
-
-
-def holds_row(device):
-    return (row_of(device) * 16) // 9 == device
-
-
-def peer(me, d):
+def peers(me):
     yh, x, z = me // 32, (me // 8) % 4, me % 8
-    dy, dx, dz = d // 32, (d // 8) % 4, d % 8
-    return ((yh + dy) % 2) * 32 + ((x + dx) % 4) * 8 + (z + dz) % 8
-
-
-def scatter(me, src, dst, slot, rows, send_sem, recv_sem):
-    def send(s, carry):
-        to = peer(me, (s * 29) % G)
+    planes = [((yh + i % 2) % 2) * 32 + ((x + i // 2) % 4) * 8 for i in range(8)]
+    return planes, z
+
+
+def for_peers(me, act):
+    planes, z = peers(me)
+    for i in range(1, 8):
+        act(planes[i] + z)
+
+    def step(s, carry):
+        at = (z + 5 * s) % 8
+        for i in range(8):
+            act(planes[i] + at)
+        return carry
+
+    lax.fori_loop(1, 8, step, 0)
+
+
+def scatter(me, src, dst, first, rows, send_sem, recv_sem):
+    landing = dst.at[pl.ds(pl.multiple_of(me * SLOT + first, 8), rows)]
+
+    def send(to):
         pltpu.make_async_remote_copy(
-            src_ref=src.at[pl.ds(pl.multiple_of(to * slot, 8), rows)],
-            dst_ref=dst.at[pl.ds(pl.multiple_of(me * slot, 8), rows)],
+            src_ref=src.at[pl.ds(pl.multiple_of(to * SLOT + first, 8), rows)],
+            dst_ref=landing,
             send_sem=send_sem,
             recv_sem=recv_sem,
             device_id={"grid": to},
             device_id_type=MESH,
         ).start()
-        return carry
-
-    lax.fori_loop(1, G, send, 0)
-
-
-def own(me, src, dst, slot, rows, sem):
-    return pltpu.make_async_copy(
-        src.at[pl.ds(pl.multiple_of(me * slot, 8), rows)],
-        dst.at[pl.ds(pl.multiple_of(me * slot, 8), rows)],
+
+    for_peers(me, send)
+
+
+def own(me, src, dst, first, rows, sem):
+    copy = pltpu.make_async_copy(
+        src.at[pl.ds(pl.multiple_of(me * SLOT + first, 8), rows)],
+        dst.at[pl.ds(pl.multiple_of(me * SLOT + first, 8), rows)],
         sem,
     )
+    copy.start()
+    return copy
 
 
 def drain(ref, rows, sem):
@@ -133,11 +141,12 @@
 
 
 def propagate(
-    psi, occ, ion, hxc, d_ref, dp_ref, h_ref, hx_ref, hxt_ref, fresh, new_pot,
+    psi_in, occ, ion_in, hxc_in, d_in, dp_in, h_in, hx_in, hxt_in, fresh_out, new_pot,
+    psi, ion, hxc, d_ref, dp_ref, h_ref, hx_ref, hxt_ref, fresh,
     out_a, in_a, out_u, in_u, out_c, in_c, vshare, pot, once, twice,
     pairs, part_s, part_r, core_s, core_r, runs_s, runs_r, from_s, from_r,
     to_rows, at_rows, back_rows, got_rows, all_s, all_r,
-    send_sems, recv_sems, own_sems, band_send, band_recv,
+    send_sems, recv_sems, own_sems, load_sems, band_send, band_recv,
 ):
     me = lax.axis_index("grid")
     band = lax.axis_index("band")
@@ -146,19 +155,38 @@
     sibling = {"band": band + 1 - 2 * core}
     others = [(line + d) % 4 for d in range(1, 4)]
 
+    loads = [
+        pltpu.make_async_copy(src, dst, load_sems.at[i])
+        for i, (src, dst) in enumerate(
+            [
+                (ion_in, ion),
+                (hxc_in, hxc),
+                (psi_in.at[0], psi),
+                (d_in, d_ref),
+                (dp_in, dp_ref),
+                (h_in, h_ref),
+                (hx_in, hx_ref),
+                (hxt_in, hxt_ref),
+            ]
+        )
+    ]
+    for load in loads:
+        load.start()
+
     barrier = pltpu.get_barrier_semaphore()
 
-    def greet(s, carry):
-        pl.semaphore_signal(barrier, inc=1, device_id={"grid": peer(me, s)}, device_id_type=MESH)
-        return carry
-
-    lax.fori_loop(1, G, greet, 0)
+    def greet(to):
+        pl.semaphore_signal(barrier, inc=1, device_id={"grid": to}, device_id_type=MESH)
+
+    for_peers(me, greet)
     pl.semaphore_signal(barrier, inc=1, device_id=sibling, device_id_type=MESH)
     for other in others:
         pl.semaphore_signal(
             barrier, inc=1, device_id={"band": 2 * other + core}, device_id_type=MESH
         )
 
+    loads[0].wait()
+    loads[1].wait()
     blocks = []
     tails = []
     for x in range(3):
@@ -171,18 +199,27 @@
     for i in range(5):
         blocks.append(jnp.concatenate([tails[2 * i], tails[2 * i + 1]], axis=1))
     for i in range(VROWS):
-        out_a[pl.ds(27 + i, G, stride=SLOT), :] = jnp.where(core == 0, blocks[i], blocks[VROWS + i])
+        out_a[pl.ds(TAIL + 9 + i, G, stride=SLOT), :] = jnp.where(core == 0, blocks[i], blocks[VROWS + i])
+
+    def at(x, kind, j):
+        return (TAIL if kind == 2 else 9 * kind) + 3 * x + j
+
+    loads[2].wait()
     for x in range(3):
         re, im = psi[0, x], psi[1, x]
         kinds = (re[:, :128], im[:, :128], jnp.concatenate([re[:, 128:], im[:, 128:]], axis=1))
         for kind in range(3):
             for j in range(3):
-                out_a[pl.ds(x * 9 + kind * 3 + j, G, stride=SLOT), :] = kinds[kind][64 * j : 64 * j + 64]
+                out_a[pl.ds(at(x, kind, j), G, stride=SLOT), :] = kinds[kind][64 * j : 64 * j + 64]
 
     pl.semaphore_wait(barrier, G + 3)
-    mine = own(me, out_a, in_a, SLOT, ROWS, own_sems.at[0])
-    mine.start()
-    scatter(me, out_a, in_a, SLOT, ROWS, send_sems.at[0], recv_sems.at[0])
+    last = 9 + VROWS
+    mine_wide = own(me, out_a, in_a, 0, WIDE, own_sems.at[0])
+    mine_tail = own(me, out_a, in_a, TAIL, last, own_sems.at[1])
+    scatter(me, out_a, in_a, 0, WIDE, send_sems.at[0], recv_sems.at[0])
+    scatter(me, out_a, in_a, TAIL, last, send_sems.at[1], recv_sems.at[1])
+    for load in loads[3:]:
+        load.wait()
 
     def inside(i, carry):
         c, x = i // 3, i % 3
@@ -196,26 +233,11 @@
 
     lax.fori_loop(0, 6, inside, 0)
 
-    mine.wait()
-    drain(in_a, ROWS, recv_sems.at[0])
-
-    for i in range(VROWS):
-        vshare[core, pl.ds(64 * i, 64), :] = in_a[pl.ds(27 + i, G, stride=SLOT), :]
-    swap = pltpu.make_async_remote_copy(
-        src_ref=vshare.at[core],
-        dst_ref=vshare.at[core],
-        send_sem=send_sems.at[3],
-        recv_sem=recv_sems.at[3],
-        device_id=sibling,
-        device_id_type=MESH,
-    )
-    swap.start()
-
-    def columns(kind):
+    def columns(ref, kind):
         return jnp.concatenate(
             [
                 jnp.concatenate(
-                    [in_a[pl.ds(x * 9 + kind * 3 + j, G, stride=SLOT), :] for j in range(3)], axis=1
+                    [ref[pl.ds(at(x, kind, j), G, stride=SLOT), :] for j in range(3)], axis=1
                 )
                 for x in range(3)
             ],
@@ -225,17 +247,35 @@
     def spread(ref, kind, value):
         for x in range(3):
             for j in range(3):
-                ref[pl.ds(x * 9 + kind * 3 + j, G, stride=BACK), :] = value[
+                ref[pl.ds(at(x, kind, j), G, stride=SLOT), :] = value[
                     64 * x : 64 * x + 64, 128 * j : 128 * j + 128
                 ]
 
     table = dp_ref[...]
-    for kind in range(3):
-        spread(out_u, kind, left_mul(table, columns(kind)))
-    mine = own(me, out_u, in_u, BACK, 27, own_sems.at[1])
-    mine.start()
-    scatter(me, out_u, in_u, BACK, 27, send_sems.at[1], recv_sems.at[1])
-
+    mine_wide.wait()
+    drain(in_a, WIDE, recv_sems.at[0])
+    for kind in range(2):
+        spread(out_u, kind, left_mul(table, columns(in_a, kind)))
+    mine_wide = own(me, out_u, in_u, 0, WIDE, own_sems.at[2])
+    scatter(me, out_u, in_u, 0, WIDE, send_sems.at[2], recv_sems.at[2])
+
+    mine_tail.wait()
+    drain(in_a, last, recv_sems.at[1])
+    spread(out_u, 2, left_mul(table, columns(in_a, 2)))
+    mine_tail = own(me, out_u, in_u, TAIL, 9, own_sems.at[3])
+    scatter(me, out_u, in_u, TAIL, 9, send_sems.at[3], recv_sems.at[3])
+
+    for i in range(VROWS):
+        vshare[core, pl.ds(64 * i, 64), :] = in_a[pl.ds(TAIL + 9 + i, G, stride=SLOT), :]
+    swap = pltpu.make_async_remote_copy(
+        src_ref=vshare.at[core],
+        dst_ref=vshare.at[core],
+        send_sem=send_sems.at[6],
+        recv_sem=recv_sems.at[6],
+        device_id=sibling,
+        device_id_type=MESH,
+    )
+    swap.start()
     swap.wait()
 
     def vblock(i):
@@ -253,28 +293,20 @@
             [jnp.concatenate([pick(3 * x + j) for j in range(3)], axis=1) for x in range(3)], axis=0
         )
 
-    def ucolumns(kind):
-        return jnp.concatenate(
-            [
-                jnp.concatenate(
-                    [out_u[pl.ds(x * 9 + kind * 3 + j, G, stride=BACK), :] for j in range(3)], axis=1
-                )
-                for x in range(3)
-            ],
-            axis=0,
-        )
-
     for kind in range(3):
-        value = ucolumns(kind) + (vcolumns(kind) - 1.0) * columns(kind)
+        value = columns(out_u, kind) + (vcolumns(kind) - 1.0) * columns(in_a, kind)
         spread(out_c, kind, left_mul(table, value))
-    mine_c = own(me, out_c, in_c, BACK, 27, own_sems.at[2])
-    mine_c.start()
-    scatter(me, out_c, in_c, BACK, 27, send_sems.at[2], recv_sems.at[2])
+    mine_c = [
+        own(me, out_c, in_c, 0, WIDE, own_sems.at[4]),
+        own(me, out_c, in_c, TAIL, 9, own_sems.at[5]),
+    ]
+    scatter(me, out_c, in_c, 0, WIDE, send_sems.at[4], recv_sems.at[4])
+    scatter(me, out_c, in_c, TAIL, 9, send_sems.at[5], recv_sems.at[5])
 
     def planes(ref, x):
         kinds = [
             jnp.concatenate(
-                [ref[pl.ds(x * 9 + kind * 3 + j, G, stride=BACK), :] for j in range(3)], axis=0
+                [ref[pl.ds(at(x, kind, j), G, stride=SLOT), :] for j in range(3)], axis=0
             )
             for kind in range(3)
         ]
@@ -282,8 +314,10 @@
         im = jnp.concatenate([kinds[1], kinds[2][:, 64:]], axis=1)
         return re, im
 
-    mine.wait()
-    drain(in_u, 27, recv_sems.at[1])
+    mine_wide.wait()
+    mine_tail.wait()
+    drain(in_u, WIDE, recv_sems.at[2])
+    drain(in_u, 9, recv_sems.at[3])
     inner = d_ref[...]
     alpha = BESSEL_ZERO + 2.0 * BESSEL_TWO
     for x in range(3):
@@ -296,8 +330,10 @@
         once[0, x] = alpha * psi[0, x] + 2.0 * BESSEL_ONE * first_im - 4.0 * BESSEL_TWO * second_re
         once[1, x] = alpha * psi[1, x] - 2.0 * BESSEL_ONE * first_re - 4.0 * BESSEL_TWO * second_im
 
-    mine_c.wait()
-    drain(in_c, 27, recv_sems.at[2])
+    for copy in mine_c:
+        copy.wait()
+    drain(in_c, WIDE, recv_sems.at[4])
+    drain(in_c, 9, recv_sems.at[5])
     table_h = h_ref[...]
     weight = occ[0]
 
@@ -318,6 +354,9 @@
         rho = weight * (re * re + im * im)
         pack(part_r, x, rho)
         pack(part_s, x, right_fine(left_fine(table_h, rho), table_h))
+
+    store = pltpu.make_async_copy(fresh, fresh_out.at[0], load_sems.at[8])
+    store.start()
 
     def swap_half(src, dst, k):
         half = pl.multiple_of((1 - core) * HALF, 8)
@@ -362,80 +401,85 @@
     swap_s.wait()
     add_half(part_s, core_s, runs_s)
     lines_s = to_lines(runs_s, from_s, 2)
+    for copy in lines_s:
+        copy.wait()
+
+    share = total(from_s)
+    for x in range(3):
+        to_rows[pl.ds(x, SHARE, stride=8), :] = share[SHARE * x : SHARE * x + SHARE]
+    planes_of, z = peers(me)
+    even = z % 2 == 0
+    extra = jnp.logical_and(me < 32, z == 1)
+    holder = jnp.logical_or(even, extra)
+    row = jnp.where(even, (me // 8) * 4 + z // 2, 32 + me // 8)
+
+    def send_row(to, r):
+        pltpu.make_async_remote_copy(
+            src_ref=to_rows.at[pl.ds(pl.multiple_of(r * 8, 8), 3)],
+            dst_ref=at_rows.at[pl.ds(pl.multiple_of(me * 8, 8), 3)],
+            send_sem=send_sems.at[7],
+            recv_sem=recv_sems.at[7],
+            device_id={"grid": to},
+            device_id_type=MESH,
+        ).start()
+
+    def send_rows(s, carry):
+        half = (z // 2 + s) % 4
+        for i in range(1, 8):
+            send_row(planes_of[i] + 2 * half, planes_of[i] // 2 + half)
+
+        @pl.when(jnp.logical_or(s > 0, z % 2 == 1))
+        def _():
+            send_row(planes_of[0] + 2 * half, planes_of[0] // 2 + half)
+
+        return carry
+
+    lax.fori_loop(0, 4, send_rows, 0)
+    for i in range(4):
+        column = ((me // 8) % 4 + i) % 4
+
+        @pl.when(me != column * 8 + 1)
+        def _():
+            send_row(column * 8 + 1, 32 + column)
+
     swap_r.wait()
     add_half(part_r, core_r, runs_r)
     lines_r = to_lines(runs_r, from_r, 5)
-    for copy in lines_s:
-        copy.wait()
-
-    share = total(from_s)
-    for x in range(3):
-        to_rows[pl.ds(x, SHARE, stride=8), :] = share[SHARE * x : SHARE * x + SHARE]
-    row = row_of(me)
-    holder = holds_row(me)
-
-    def send_row(s, carry):
-        to = peer(me, (s * 29) % G)
-
-        @pl.when(holds_row(to))
-        def _():
-            pltpu.make_async_remote_copy(
-                src_ref=to_rows.at[pl.ds(pl.multiple_of(row_of(to) * 8, 8), 3)],
-                dst_ref=at_rows.at[pl.ds(pl.multiple_of(me * 8, 8), 3)],
-                send_sem=send_sems.at[4],
-                recv_sem=recv_sems.at[4],
-                device_id={"grid": to},
-                device_id_type=MESH,
-            ).start()
-
-        return carry
-
-    lax.fori_loop(1, G, send_row, 0)
-
-    for copy in lines_r:
-        copy.wait()
 
     def gather_start(ref, k):
-        mine = ref.at[pl.ds(pl.multiple_of(core * HALF + line * UNIT, 8), UNIT)]
-        copies = []
-        for i, other in enumerate(others):
+        def push(other, device, sem):
+            unit = ref.at[pl.ds(pl.multiple_of(core * HALF + other * UNIT, 8), UNIT)]
             copy = pltpu.make_async_remote_copy(
-                src_ref=mine,
-                dst_ref=mine,
-                send_sem=band_send.at[k + i],
-                recv_sem=band_recv.at[k + i],
-                device_id={"band": 2 * other + core},
+                src_ref=unit,
+                dst_ref=unit,
+                send_sem=band_send.at[sem],
+                recv_sem=band_recv.at[sem],
+                device_id=device,
                 device_id_type=MESH,
             )
             copy.start()
-            copies.append(copy)
-        return copies
-
-    def gather_cores(ref, k):
-        half = ref.at[pl.ds(pl.multiple_of(core * HALF, 8), HALF)]
-        copy = pltpu.make_async_remote_copy(
-            src_ref=half,
-            dst_ref=half,
-            send_sem=band_send.at[k],
-            recv_sem=band_recv.at[k],
-            device_id=sibling,
-            device_id_type=MESH,
-        )
-        copy.start()
-        return copy
+            return copy
+
+        copies = [push(line, {"band": 2 * other + core}, k + i) for i, other in enumerate(others)]
+        copies.append(push(line, sibling, k + 3))
+        return push, copies, k + 4
+
+    def gather_finish(started):
+        push, copies, k = started
+        passed = []
+        for i in range(3):
+            copies[i].wait()
+            passed.append(push(others[2 - i], sibling, k + i))
+        for copy in [copies[3]] + passed:
+            copy.wait()
 
     place = pl.ds(pl.multiple_of(core * HALF + line * UNIT, 8), UNIT)
-    rho_share = total(from_r)
-    root = jnp.exp(jnp.log(jnp.maximum(rho_share, 1e-37)) * (1.0 / 3.0))
-    all_r[place, :] = -XC_FACTOR * jnp.where(rho_share > 0, root, 0.0)
-    gather_r = gather_start(all_r, 8)
-
     @pl.when(holder)
     def _():
         at_rows[pl.ds(pl.multiple_of(me * 8, 8), 8), :] = to_rows[
             pl.ds(pl.multiple_of(row * 8, 8), 8), :
         ]
-        drain(at_rows, 3, recv_sems.at[4])
+        drain(at_rows, 3, recv_sems.at[7])
         lines = jnp.concatenate([at_rows[pl.ds(x, G, stride=8), :] for x in range(3)], axis=0)
         spectrum = left_fine(hx_ref[...], lines)
         kx = lax.broadcasted_iota(jnp.int32, (N, 128), 0)
@@ -452,19 +496,17 @@
         for x in range(3):
             back_rows[pl.ds(x, G, stride=8), :] = result[64 * x : 64 * x + 64]
 
-        def send_back(s, carry):
-            to = peer(me, (s * 29) % G)
+        def send_back(to):
             pltpu.make_async_remote_copy(
                 src_ref=back_rows.at[pl.ds(pl.multiple_of(to * 8, 8), 3)],
                 dst_ref=got_rows.at[pl.ds(pl.multiple_of(row * 8, 8), 3)],
-                send_sem=send_sems.at[5],
-                recv_sem=recv_sems.at[5],
+                send_sem=send_sems.at[8],
+                recv_sem=recv_sems.at[8],
                 device_id={"grid": to},
                 device_id_type=MESH,
             ).start()
-            return carry
-
-        lax.fori_loop(1, G, send_back, 0)
+
+        for_peers(me, send_back)
         got_rows[pl.ds(pl.multiple_of(row * 8, 8), 8), :] = back_rows[
             pl.ds(pl.multiple_of(me * 8, 8), 8), :
         ]
@@ -480,19 +522,21 @@
             span = to_rows.at[pl.ds(0, 36 * 3)]
             pltpu.make_async_copy(span, span, sem).wait()
 
-    for copy in gather_r:
+    for copy in lines_r:
         copy.wait()
-    cores_r = gather_cores(all_r, 11)
-
-    drain_rows(recv_sems.at[5])
+    rho_share = total(from_r)
+    root = jnp.exp(jnp.log(jnp.maximum(rho_share, 1e-37)) * (1.0 / 3.0))
+    all_r[place, :] = -XC_FACTOR * jnp.where(rho_share > 0, root, 0.0)
+    gather_r = gather_start(all_r, 8)
+
+    drain_rows(recv_sems.at[8])
     for x in range(3):
         all_s[pl.ds(pl.multiple_of(core * HALF + line * UNIT + SHARE * x, 8), SHARE), :] = got_rows[
             pl.ds(x, SHARE, stride=8), :
         ]
-    for copy in gather_start(all_s, 12):
-        copy.wait()
-    cores_r.wait()
-    gather_cores(all_s, 15).wait()
+    gather_s = gather_start(all_s, 15)
+    gather_finish(gather_r)
+    gather_finish(gather_s)
 
     def unpack(ref, x):
         wide = []
@@ -508,14 +552,31 @@
         spectrum = unpack(all_s, x)
         new_pot[x] = right_mul(left_mul(table_h, spectrum), table_h) + unpack(all_r, x)
 
-    drain(out_a, ROWS, send_sems.at[0])
-    drain(out_u, 27, send_sems.at[1])
-    drain(out_c, 27, send_sems.at[2])
-    drain_rows(send_sems.at[4])
+    drain(out_a, WIDE, send_sems.at[0])
+    drain(out_a, last, send_sems.at[1])
+    for k, ref in ((2, out_u), (4, out_c)):
+        drain(ref, WIDE, send_sems.at[k])
+        drain(ref, 9, send_sems.at[k + 1])
+    drain_rows(send_sems.at[7])
+    store.wait()
 
     @pl.when(holder)
     def _():
-        drain(back_rows, 3, send_sems.at[5])
+        drain(back_rows, 3, send_sems.at[8])
+
+
+def hand_over(fresh, pot, fresh_out, pot_out, fresh_held, pot_held, in_sems, out_sems):
+    moves = [(fresh.at[0, c, x], fresh_held.at[c, x], fresh_out.at[0, c, x]) for c in range(2) for x in range(3)]
+    moves += [(pot.at[x], pot_held.at[x], pot_out.at[x]) for x in range(3)]
+    loads = [pltpu.make_async_copy(src, held, in_sems.at[i]) for i, (src, held, _) in enumerate(moves)]
+    stores = [pltpu.make_async_copy(held, dst, out_sems.at[i]) for i, (_, held, dst) in enumerate(moves)]
+    for load in loads:
+        load.start()
+    for load, store in zip(loads, stores):
+        load.wait()
+        store.start()
+    for store in stores:
+        store.wait()
 
 
 def local(orbitals, occupations, ion, hxc):
@@ -524,20 +585,31 @@
     order = np.arange(N)
     order = 3 * (order % G) + order // G
     vmem = pl.BlockSpec(memory_space=pltpu.VMEM)
+    hbm = pl.BlockSpec(memory_space=pl.ANY)
     f32 = jnp.float32
+    shapes = (jax.ShapeDtypeStruct((1, 2, 3, N, N), f32), jax.ShapeDtypeStruct((3, N, N), f32))
     slots = lambda rows: pltpu.VMEM((rows, 128), f32)
     fresh, new_pot = pl.pallas_call(
         propagate,
-        out_shape=(jax.ShapeDtypeStruct((2, 3, N, N), f32), jax.ShapeDtypeStruct((3, N, N), f32)),
-        in_specs=[vmem, pl.BlockSpec(memory_space=pltpu.SMEM)] + [vmem] * 7,
-        out_specs=(vmem, vmem),
+        out_shape=shapes,
+        in_specs=[hbm, pl.BlockSpec(memory_space=pltpu.SMEM)] + [hbm] * 7,
+        out_specs=(hbm, vmem),
         scratch_shapes=[
+            pltpu.VMEM((2, 3, N, N), f32),
+            pltpu.VMEM((3, N, N), f32),
+            pltpu.VMEM((3, N, N), f32),
+            pltpu.VMEM((2, N, N), jnp.bfloat16),
+            pltpu.VMEM((2, N, N), jnp.bfloat16),
+            pltpu.VMEM((3, N, N), jnp.bfloat16),
+            pltpu.VMEM((3, N, N), jnp.bfloat16),
+            pltpu.VMEM((2, N, N), jnp.bfloat16),
+            pltpu.VMEM((2, 3, N, N), f32),
             slots(G * SLOT),
             slots(G * SLOT),
-            slots(G * BACK),
-            slots(G * BACK),
-            slots(G * BACK),
-            slots(G * BACK),
+            slots(G * SLOT),
+            slots(G * SLOT),
+            slots(G * SLOT),
+            slots(G * SLOT),
             pltpu.VMEM((2, VROWS * 64, 128), f32),
             pltpu.VMEM((3, N, N), f32),
             pltpu.VMEM((2, 3, N, N), f32),
@@ -557,18 +629,19 @@
             slots(SHARE * 8),
             slots(2 * HALF),
             slots(2 * HALF),
+            pltpu.SemaphoreType.DMA((9,)),
+            pltpu.SemaphoreType.DMA((9,)),
             pltpu.SemaphoreType.DMA((6,)),
-            pltpu.SemaphoreType.DMA((6,)),
-            pltpu.SemaphoreType.DMA((3,)),
-            pltpu.SemaphoreType.DMA((16,)),
-            pltpu.SemaphoreType.DMA((16,)),
+            pltpu.SemaphoreType.DMA((9,)),
+            pltpu.SemaphoreType.DMA((22,)),
+            pltpu.SemaphoreType.DMA((22,)),
         ],
         compiler_params=pltpu.CompilerParams(
             collective_id=1, has_side_effects=True, vmem_limit_bytes=56 << 20
         ),
         name="propagate",
     )(
-        orbitals[0],
+        orbitals,
         occupations,
         ion,
         hxc,
@@ -578,7 +651,19 @@
         split_table(cas[:, order], 3),
         split_table(cas[:, order].T),
     )
-    return fresh[None], new_pot
+    return pl.pallas_call(
+        hand_over,
+        out_shape=shapes,
+        in_specs=[hbm, hbm],
+        out_specs=(hbm, hbm),
+        scratch_shapes=[
+            pltpu.VMEM((2, 3, N, N), f32),
+            pltpu.VMEM((3, N, N), f32),
+            pltpu.SemaphoreType.DMA((9,)),
+            pltpu.SemaphoreType.DMA((9,)),
+        ],
+        name="hand_over",
+    )(fresh, new_pot)
 
 
 def solution(mesh):

time: 144 us -> 130 us (0.903)
  Pallas kernels: 139 us -> 128 us
  local copies, waits for them, and re-layouts: 3.3 us -> 0 us
    pallas_call x1 -> x2, Pallas kernels: 139 us -> 128 us  [the longest x1 126 us: local(): pl.pallas_call(propagate, out_shape=shapes, in_specs=[hbm, pl.BlockSpec(m...]
    unnamed x4 -> x0, local copies, waits for them, and re-layouts: 3.3 us -> none
where the time goes in v3:
time: 130 us
  Pallas kernels  128 us (98%)
    pallas_call x1, Pallas kernels, local(): pl.pallas_call(propagate, out_shape=shapes, in_specs=[hbm, pl.BlockSpec(m...  126 us

profile of v3, /device:TPU:1, one launch (start us, length us, event | category | flops | bytes accessed | tf_op | source)
XLA Modules:
  0.0 129.8 jit_solution(12964444607754770409)
XLA Ops:
  1.3 126.1 %propagate.1 = (f32[1,2,3,192,192]{4,3,2,1,0:T(8,128)}, f32[3,192,192]{2,1,0:T(8,128)}) custom-call(f32[1,2,3,192,192]{4,3,2,1,0:T(8,128)} %psi_in.1, f32[1]{0:T(128)S(6)} %copy.11.occ, f32[3,192,192]{2,1,0:T(8,128)} %ion_in.1, f32[3,192,192]{2,1,0:T(8,128)} %hxc_in.1, bf16[2,192,192]{2,1,0:T(8,128)(2,1)} %constant.10.clone.d_in, ...), custom_call_target="tpu_custom_call" | custom-call | tf_op jit(solution)/shard_map/propagate/pallas_call | solution.py:592
  127.4 2.4 %hand_over.1 = (f32[1,2,3,192,192]{4,3,2,1,0:T(8,128)}, f32[3,192,192]{2,1,0:T(8,128)}) custom-call(f32[1,2,3,192,192]{4,3,2,1,0:T(8,128)} %get-tuple-element.4.fresh, f32[3,192,192]{2,1,0:T(8,128)} %get-tuple-element.5.pot), custom_call_target="tpu_custom_call" | custom-call | tf_op jit(solution)/shard_map/hand_over/pallas_call | solution.py:654

commit v4 on v3

--- a/solution.py
+++ b/solution.py
@@ -159,9 +159,9 @@
         pltpu.make_async_copy(src, dst, load_sems.at[i])
         for i, (src, dst) in enumerate(
             [
+                (psi_in.at[0], psi),
                 (ion_in, ion),
                 (hxc_in, hxc),
-                (psi_in.at[0], psi),
                 (d_in, d_ref),
                 (dp_in, dp_ref),
                 (h_in, h_ref),
@@ -185,8 +185,28 @@
             barrier, inc=1, device_id={"band": 2 * other + core}, device_id_type=MESH
         )
 
+    def at(x, kind, j):
+        return (TAIL if kind == 2 else 9 * kind) + 3 * x + j
+
     loads[0].wait()
+    for x in range(3):
+        for kind in range(2):
+            for j in range(3):
+                out_a[pl.ds(at(x, kind, j), G, stride=SLOT), :] = psi[
+                    kind, x, 64 * j : 64 * j + 64, :128
+                ]
+
+    pl.semaphore_wait(barrier, G + 3)
+    last = 9 + VROWS
+    mine_wide = own(me, out_a, in_a, 0, WIDE, own_sems.at[0])
+    scatter(me, out_a, in_a, 0, WIDE, send_sems.at[0], recv_sems.at[0])
+
+    for x in range(3):
+        value = jnp.concatenate([psi[0, x, :, 128:], psi[1, x, :, 128:]], axis=1)
+        for j in range(3):
+            out_a[pl.ds(at(x, 2, j), G, stride=SLOT), :] = value[64 * j : 64 * j + 64]
     loads[1].wait()
+    loads[2].wait()
     blocks = []
     tails = []
     for x in range(3):
@@ -199,24 +219,10 @@
     for i in range(5):
         blocks.append(jnp.concatenate([tails[2 * i], tails[2 * i + 1]], axis=1))
     for i in range(VROWS):
-        out_a[pl.ds(TAIL + 9 + i, G, stride=SLOT), :] = jnp.where(core == 0, blocks[i], blocks[VROWS + i])
-
-    def at(x, kind, j):
-        return (TAIL if kind == 2 else 9 * kind) + 3 * x + j
-
-    loads[2].wait()
-    for x in range(3):
-        re, im = psi[0, x], psi[1, x]
-        kinds = (re[:, :128], im[:, :128], jnp.concatenate([re[:, 128:], im[:, 128:]], axis=1))
-        for kind in range(3):
-            for j in range(3):
-                out_a[pl.ds(at(x, kind, j), G, stride=SLOT), :] = kinds[kind][64 * j : 64 * j + 64]
-
-    pl.semaphore_wait(barrier, G + 3)
-    last = 9 + VROWS
-    mine_wide = own(me, out_a, in_a, 0, WIDE, own_sems.at[0])
+        out_a[pl.ds(TAIL + 9 + i, G, stride=SLOT), :] = jnp.where(
+            core == 0, blocks[i], blocks[VROWS + i]
+        )
     mine_tail = own(me, out_a, in_a, TAIL, last, own_sems.at[1])
-    scatter(me, out_a, in_a, 0, WIDE, send_sems.at[0], recv_sems.at[0])
     scatter(me, out_a, in_a, TAIL, last, send_sems.at[1], recv_sems.at[1])
     for load in loads[3:]:
         load.wait()
@@ -536,8 +542,6 @@
         ]
     gather_s = gather_start(all_s, 15)
     gather_finish(gather_r)
-    gather_finish(gather_s)
-
     def unpack(ref, x):
         wide = []
         for b in range(8):
@@ -549,8 +553,11 @@
         return jnp.concatenate([jnp.concatenate(wide, axis=0), tail], axis=1)
 
     for x in range(3):
+        new_pot[x] = unpack(all_r, x)
+    gather_finish(gather_s)
+    for x in range(3):
         spectrum = unpack(all_s, x)
-        new_pot[x] = right_mul(left_mul(table_h, spectrum), table_h) + unpack(all_r, x)
+        new_pot[x] = right_mul(left_mul(table_h, spectrum), table_h) + new_pot[x]
 
     drain(out_a, WIDE, send_sems.at[0])
     drain(out_a, last, send_sems.at[1])

time: 130 us -> 130 us (level)
  no operation moved by 1% of the time
where the time goes in v4:
time: 130 us
  Pallas kernels  129 us (99%)
    pallas_call x1, Pallas kernels, local(): pl.pallas_call(propagate, out_shape=shapes, in_specs=[hbm, pl.BlockSpec(m...  126 us

profile of v4, /device:TPU:1, one launch (start us, length us, event | category | flops | bytes accessed | tf_op | source)
XLA Modules:
  0.0 129.8 jit_solution(16023892897188069887)
XLA Ops:
  1.3 126.2 %propagate.1 = (f32[1,2,3,192,192]{4,3,2,1,0:T(8,128)}, f32[3,192,192]{2,1,0:T(8,128)}) custom-call(f32[1,2,3,192,192]{4,3,2,1,0:T(8,128)} %psi_in.1, f32[1]{0:T(128)S(6)} %copy.11.occ, f32[3,192,192]{2,1,0:T(8,128)} %ion_in.1, f32[3,192,192]{2,1,0:T(8,128)} %hxc_in.1, bf16[2,192,192]{2,1,0:T(8,128)(2,1)} %constant.10.clone.d_in, ...), custom_call_target="tpu_custom_call" | custom-call | tf_op jit(solution)/shard_map/propagate/pallas_call | solution.py:599
  127.5 2.4 %hand_over.1 = (f32[1,2,3,192,192]{4,3,2,1,0:T(8,128)}, f32[3,192,192]{2,1,0:T(8,128)}) custom-call(f32[1,2,3,192,192]{4,3,2,1,0:T(8,128)} %get-tuple-element.4.fresh, f32[3,192,192]{2,1,0:T(8,128)} %get-tuple-element.5.pot), custom_call_target="tpu_custom_call" | custom-call | tf_op jit(solution)/shard_map/hand_over/pallas_call | solution.py:661
